TPU v7x, 256 devices: a whole 4x4x8 slice. The times are simulated.
256 devices in a mesh: pb: 4 (over z_lo), vert: 64 (over z_hi, y, x, core).
Axes of the slice: x: 4, y: 4, z: 8 (z_hi: 2, z_lo: 4; z = z_hi * 4 + z_lo), core: 2. Of those that a mesh axis runs over, the one named last changes fastest.
Arguments:
- queries: float32 [8192, 768], P('pb'), may hold values from -16 to 16
- views: float32 [65536, 768], P(('vert', 'pb')), may hold values from -4 to 4
- positives: int32 [8192], P('pb'), may hold values from 0 to 65535
- query_weight: float32 [8192], P('pb'), may hold values from 0.3 to 3
- owners: int32 [65536], P('vert'), may hold values from 0 to 8191
- view_weight: float32 [65536], P('vert'), may hold values from 0.3 to 3
- view_kinds: int32 [65536], P('vert'), may hold values from 0 to 2
- kind_scale: float32 [3], replicated, may hold values from 2 to 8
Outputs:
- grad_q: float32 [8192, 768], P(('pb', 'vert'))
- grad_v: float32 [65536, 768], P(('vert', 'pb'))
- type_grad: float32 [3], replicated
All inputs are finite; a program needn't handle non-finite values.
Results may differ from a plain program's by a relative error of at most 0.003.
The roundings to bfloat16 on the way count: a program that leaves them out, or rounds other values in their place, can miss the bound.
Values may be sent and summed in bfloat16 or wider, within the bound.
A program may use at most 64 MiB of HBM per device.

v0:
```python
import math

import jax
import jax.numpy as jnp
from jax import lax
from jax.sharding import PartitionSpec as P


def on_device(queries, views, positives, query_weight, owners, view_weight, view_kinds, kind_scale):
    tile_rows = queries.shape[0]
    feature_width = queries.shape[1]
    v_half = lax.all_gather(views.astype(jnp.bfloat16), "pb", axis=0, tiled=True)
    tile_cols = v_half.shape[0]
    q_half = queries.astype(jnp.bfloat16)
    row_anchor = lax.axis_index("pb") * tile_rows
    col_anchor = lax.axis_index("vert") * tile_cols
    kind_ids = jnp.arange(kind_scale.shape[0], dtype=jnp.int32)
    kind_hot = (view_kinds[:, None] == kind_ids[None, :]).astype(jnp.float32)
    col_scale = jnp.sum(kind_hot * kind_scale[None, :], axis=1)
    block_rows = math.gcd(tile_rows, 512)
    block_count = tile_rows // block_rows
    q_blocks = q_half.reshape(block_count, block_rows, feature_width)
    col_ids = jnp.arange(tile_cols, dtype=jnp.int32)

    def scored(q_block):
        products = lax.dot_general(
            q_block, v_half, (((1,), (1,)), ((), ())), preferred_element_type=jnp.float32
        )
        return products * col_scale[None, :]

    def first_pass(running, q_block):
        col_peak, col_total = running
        scores = scored(q_block)
        row_peak = jnp.max(scores, axis=1)
        row_total = jnp.sum(jnp.exp(scores - row_peak[:, None]), axis=1)
        merged_max = jnp.maximum(col_peak, jnp.max(scores, axis=0))
        col_total = col_total * jnp.exp(col_peak - merged_max) + jnp.sum(
            jnp.exp(scores - merged_max[None, :]), axis=0
        )
        return ((merged_max, col_total), (row_peak, row_total, scores))

    initial = (jnp.full((tile_cols,), -jnp.inf, jnp.float32), jnp.zeros((tile_cols,), jnp.float32))
    (col_peak, col_total), (row_peak, row_total, score_blocks) = lax.scan(
        first_pass, initial, q_blocks
    )
    row_peak = row_peak.reshape(tile_rows)
    row_total = row_total.reshape(tile_rows)
    row_max = lax.pmax(row_peak, "vert")
    row_sum = lax.psum(row_total * jnp.exp(row_peak - row_max), "vert")
    col_max = lax.pmax(col_peak, "pb")
    col_sum = lax.psum(col_total * jnp.exp(col_peak - col_max), "pb")
    row_lse = row_max + jnp.log(row_sum)
    col_lse = col_max + jnp.log(col_sum)
    pos_local = positives - col_anchor
    own_local = owners - row_anchor
    first_rows = jnp.arange(block_count, dtype=jnp.int32) * block_rows

    def second_pass(col_terms, operands):
        scores, lse_block, weight_block, pos_block, first_row = operands
        pos_hot = (pos_block[:, None] == col_ids[None, :]).astype(jnp.float32)
        row_ids = first_row + jnp.arange(block_rows, dtype=jnp.int32)
        own_hot = (row_ids[:, None] == own_local[None, :]).astype(jnp.float32)
        grad = weight_block[:, None] * (jnp.exp(scores - lse_block[:, None]) - pos_hot)
        grad = grad + view_weight[None, :] * (jnp.exp(scores - col_lse[None, :]) - own_hot)
        col_terms = col_terms + jnp.sum(grad * scores, axis=0)
        return (col_terms, (grad * col_scale[None, :]).astype(jnp.bfloat16))

    operands = (
        score_blocks,
        row_lse.reshape(block_count, block_rows),
        query_weight.reshape(block_count, block_rows),
        pos_local.reshape(block_count, block_rows),
        first_rows,
    )
    col_terms, half_blocks = lax.scan(second_pass, jnp.zeros((tile_cols,), jnp.float32), operands)
    half_tile = half_blocks.reshape(tile_rows, tile_cols)
    grad_q = lax.psum_scatter(
        jnp.dot(half_tile, v_half, preferred_element_type=jnp.float32),
        "vert",
        scatter_dimension=0,
        tiled=True,
    )
    grad_v = lax.psum_scatter(
        lax.dot_general(
            half_tile, q_half, (((0,), (0,)), ((), ())), preferred_element_type=jnp.float32
        ),
        "pb",
        scatter_dimension=0,
        tiled=True,
    )
    per_kind = jnp.sum(kind_hot * col_terms[:, None], axis=0)
    summed = lax.psum(per_kind, ("pb", "vert"))
    type_grad = summed / (tile_rows * lax.axis_size("pb"))
    return (grad_q, grad_v, type_grad)


def solution(mesh):
    in_specs = (
        P("pb", None),
        P(("vert", "pb"), None),
        P("pb"),
        P("pb"),
        P("vert"),
        P("vert"),
        P("vert"),
        P(),
    )
    out_specs = (P(("pb", "vert"), None), P(("vert", "pb"), None), P())
    return jax.shard_map(
        on_device, mesh=mesh, in_specs=in_specs, out_specs=out_specs, check_vma=False
    )
```

profile of v0, /device:TPU:2, one launch (start us, length us, event | category | flops | bytes accessed | tf_op | source)
XLA Modules:
  0.0 797.5 jit_solution(6420761253075176721)
XLA Ops:
  7.2 1.9 convert_element_type.36
  9.3 4.8 convert_element_type.35
  14.3 40.8 %all-gather.2.cloned.1.call-done = bf16[1024,768]{1,0:T(8,128)(2,1)} async-done(((bf16[256,768]{1,0:T(8,128)(2,1)}), bf16[1024,768]{1,0:T(8,128)(2,1)}) %all-gather.2.cloned.1.call-update) | async-done | bytes 1572880 | tf_op jit(solution)/shard_map/all_gather | solution.py:12
  55.1 20.3 %while.33 = (s32[]{:T(128)}, f32[1024]{0:T(1024)S(1)}, f32[1024]{0:T(1024)S(1)}, f32[4,512]{1,0:T(4,128)S(1)}, f32[4,512]{1,0:T(4,128)S(1)}, /*index=5*/f32[4,51...) while((s32[]{:T(128)}, f32[1024]{0:T(1024)S(1)}, ...), condition=%wide.region_6.7_spmd.clone, body=%wide.region_1.6_spmd.clone.sunk | while | flops 808980480 | bytes 10820736 | solution.py:43
  55.1 2.8 fusion.29
  57.8 0.7 exponential_reduce_fusion.3
  58.6 1.5 bitcast_dynamic-update-slice_fusion.2
  60.2 2.8 fusion.29
  63.7 1.4 bitcast_dynamic-update-slice_fusion.2
  65.2 2.8 fusion.29
  68.8 1.5 bitcast_dynamic-update-slice_fusion.2
  70.3 2.8 fusion.29
  73.8 1.5 bitcast_dynamic-update-slice_fusion.2
  75.4 9.7 %pmax.15 = f32[1024]{0:T(1024)S(1)} all-reduce(f32[1024]{0:T(1024)S(1)} %get-tuple-element.128), channel_id=1, replica_groups=mesh['pb'=4,'vert'=64] {'pb'}, use_global_device_ids=true, to_apply=%region_9.10 | all-reduce | flops 1024 | bytes 8192 | tf_op jit(solution)/shard_map/pmax | solution.py:50
  85.1 9.1 %psum.22 = f32[1024]{0:T(1024)S(1)} all-reduce(f32[1024]{0:T(1024)S(1)} %exponential_multiply_fusion.1), channel_id=1, replica_groups=mesh['pb'=4,'vert'=64] {'pb'}, use_global_device_ids=true, to_apply=%region_10.11 | all-reduce | flops 1024 | bytes 8192 | tf_op jit(solution)/shard_map/psum | solution.py:51
  94.1 197.9 %pmax.14 = f32[2048]{0:T(1024)S(1)} all-reduce(f32[2048]{0:T(1024)S(1)} %bitcast.78), channel_id=1, replica_groups=mesh['pb'=4,'vert'=64] {'vert'}, use_global_device_ids=true, to_apply=%region_7.8 | all-reduce | flops 2048 | bytes 16384 | tf_op jit(solution)/shard_map/pmax | solution.py:48
  292.1 203.0 %psum.21 = f32[2048]{0:T(1024)S(1)} all-reduce(f32[2048]{0:T(1024)S(1)} %exponential_multiply_fusion), channel_id=1, replica_groups=mesh['pb'=4,'vert'=64] {'vert'}, use_global_device_ids=true, to_apply=%region_8.9 | all-reduce | flops 2048 | bytes 16384 | tf_op jit(solution)/shard_map/psum | solution.py:49
  495.2 30.7 %while.34 = (s32[]{:T(128)}, f32[1024]{0:T(1024)S(1)}, bf16[4,512,1024]{2,1,0:T(8,128)(2,1)}, f32[4,512]{1,0:T(4,128)S(1)}, f32[4,512,1024]{2,1,0:T(8,128)}, /*i...) while((s32[]{:T(128)}, f32[1024]{0:T(1024)S(1)}, ...), condition=%wide.region_13.14_spmd.clone.clone, body=%wide.region_11.13_spmd.clone.clone.sunk | while | flops 13633027 | bytes 5319339 | solution.py:75
  495.8 1.0 iota_add_fusion.2
  496.8 3.7 fusion.32
  500.5 2.6 fusion.31
  504.4 3.6 fusion.32
  508.0 2.6 fusion.31
  512.0 3.6 fusion.32
  515.6 2.6 fusion.31
  519.5 3.6 fusion.32
  523.2 2.6 fusion.31
  525.8 7.5 fusion.17
  533.4 1.3 copy-done.7
  534.7 8.3 %fusion.16 = f32[2048,768]{1,0:T(8,128)} fusion(bf16[2048,1024]{1,0:T(8,128)(2,1)} %bitcast.84, bf16[1024,768]{1,0:T(8,128)(2,1)S(1)} %copy-done.7), kind=kOutput, calls=%fused_computation.43 | convolution fusion | flops 3221225472 | bytes 12058624 | tf_op jit(solution)/shard_map/dot_general | solution.py:78
  543.1 87.2 %psum.23 = f32[3]{0:T(128)S(1)} all-reduce(f32[3]{0:T(128)S(1)} %select_reduce_fusion), channel_id=1, replica_groups=mesh['pb'=4,'vert'=64] {'pb','vert'}, use_global_device_ids=true, to_apply=%region_17.18 | all-reduce | flops 3 | bytes 24 | tf_op jit(solution)/shard_map/psum | solution.py:92
  630.9 160.2 %reduce-scatter.3.cloned.1.call-done = f32[32,768]{1,0:T(8,128)} async-done(((f32[2048,768]{1,0:T(8,128)}), f32[32,768]{1,0:T(8,128)}) %reduce-scatter.3.cloned.1.call-update) | async-done | bytes 98320 | tf_op jit(solution)/shard_map/reduce_scatter | solution.py:77
  (86 shorter events, 8.0 us)
Async XLA Ops:
  7.2 47.9 %all-gather.2.cloned.1.call-start = ((), (), s32[]{:S(2)}) async-start(), calls=%async_computation.2 | async-start | bytes 1966080 | tf_op jit(solution)/shard_map/all_gather | solution.py:12
  9.2 621.7 %reduce-scatter.5.cloned.1.call-start = ((), (), s32[]{:S(2)}) async-start(), calls=%async_computation.4 | async-start | bytes 3932160 | tf_op jit(solution)/shard_map/reduce_scatter | solution.py:83
  9.3 4.8 copy-start.3
  9.3 4.8 copy-start.4
  9.3 4.9 copy-start.2
  9.3 4.9 copy-start.6
  9.3 5.0 copy-start.5
  55.1 440.1 %copy-start.1 = (f32[1024]{0:T(1024)S(1)}, f32[1024]{0:T(1024)}, u32[]{:S(2)}) copy-start(f32[1024]{0:T(1024)} %param.17) | copy-start | bytes 12292
  495.2 30.7 %copy-start = (bf16[4,512,768]{2,1,0:T(8,128)(2,1)S(1)}, bf16[4,512,768]{2,1,0:T(8,128)(2,1)}, u32[]{:S(2)}) copy-start(bf16[4,512,768]{2,1,0:T(8,128)(2,1)} %get-tuple-element.506) | copy-start | bytes 9437188
  533.3 1.4 copy-start.7
  533.3 257.7 %reduce-scatter.3.cloned.1.call-start = ((), (), s32[]{:S(2)}) async-start(), calls=%async_computation.3 | async-start | bytes 6389760 | tf_op jit(solution)/shard_map/reduce_scatter | solution.py:77
Sparse Core Ops, SparseCore 0:
  10.4 44.6 all-gather.1
  533.4 69.1 reduce-scatter.4
  609.0 181.9 reduce-scatter.2
where the time goes:
time: 798 us
  blocking collectives  507 us (64%)
  waiting for transfers between devices  201 us (25%)
  other arithmetic  38.4 us (5%)
  matrix products  26.8 us (3%)
  between operations  14 us (2%)
  local copies, waits for them, and re-layouts  10 us (1%)
    psum x1, blocking collectives, on_device(): row_sum = lax.psum(row_total * jnp.exp(row_peak - row_max), 'vert')  203 us
    pmax x1, blocking collectives, on_device(): row_max = lax.pmax(row_peak, 'vert')  198 us
    reduce_scatter x1, waiting for transfers between devices, on_device(): lax.psum_scatter(jnp.dot(half_tile, v_half, preferred_element_type=jnp.fl...  160 us
    psum x1, blocking collectives, on_device(): summed = lax.psum(per_kind, ('pb', 'vert'))  87.2 us
    all_gather x1, waiting for transfers between devices, on_device(): lax.all_gather(views.astype(jnp.bfloat16), 'pb', axis=0, tiled=True)  40.8 us
  transfers between devices with their start and end apart: 3, of which 2 were waited for; matrix products, arithmetic and copies ran while one was open for 2% of the time, Pallas kernels for 0%

commit v1 on v0

v1 whole, which is shorter than its diff:
```python
import functools
import math

import jax
import jax.numpy as jnp
from jax import lax
from jax.experimental import pallas as pl
from jax.experimental.pallas import tpu as pltpu
from jax.sharding import PartitionSpec as P

MESH = pl.DeviceIdType.MESH
LOG2E = math.log2(math.e)
LN2 = math.log(2.0)
NPB = 4
NX = 4
NY = 4
NA = 8
NB = 8
CHUNK = 256
F32 = jnp.float32
BF16 = jnp.bfloat16


def kernel(total_queries, kscale_ref, views_ref, q_hbm, pos_ref, qw_ref, own_ref, vw_ref, kind_ref,
           gq_out, gv_out, tg_out,
           qb, qt, vb, S, H, stat, arep, qwrep, posrep, gq, gvt, zs, zrl, zrr, crecv,
           sa1, sb1, ra1, rb1, sa2, sb2, ra2, rb2, acca, accb, zra, zrb,
           colst, rowa, rowb, colfin, rowfin, ta, tb, tp,
           qsem, ag_send, ag_recv, col_send, col_recv, row_send, row_recv, t_send, t_recv,
           c_send, c_recv, x_send, x_recv, z_send, zl_recv, zr_recv):
    p = lax.axis_index("pb")
    v = lax.axis_index("vert")
    core = v % 2
    x = (v // 2) % NX
    y = (v // (2 * NX)) % NY
    zh = v // (2 * NX * NY)
    a_me = v % NA
    b_me = v // NA
    rows, width = qb.shape
    nchunk = rows // CHUNK
    vcols = vb.shape[1]
    groups = nchunk * 4
    gpc = groups // nchunk

    def vert_of(zh_, y_, x_, c_):
        return ((zh_ * NY + y_) * NX + x_) * 2 + c_

    def remote(src, dst, ssem, rsem, dev):
        return pltpu.make_async_remote_copy(src_ref=src, dst_ref=dst, send_sem=ssem, recv_sem=rsem,
                                            device_id=dev, device_id_type=MESH)

    for r in range(nchunk):
        pltpu.make_async_copy(q_hbm.at[pl.ds(r * gpc, gpc)], gq.at[pl.ds(r * gpc, gpc)], qsem.at[r]).start()

    peers = [((p + d) % NPB, v) for d in range(1, NPB)]
    peers_a = [(p, b_me * NA + (a_me + d) % NA) for d in range(1, NA)]
    peers_b = [(p, ((b_me + d) % NB) * NA + a_me) for d in range(1, NB)]
    barrier = pltpu.get_barrier_semaphore()
    for dev in peers + peers_a + peers_b:
        pl.semaphore_signal(barrier, inc=1, device_id=dev, device_id_type=MESH)
    vb[p] = views_ref[...].astype(BF16)
    pl.semaphore_wait(barrier, len(peers) + len(peers_a) + len(peers_b))

    def send_right(k, s):
        return remote(vb.at[k], vb.at[k], ag_send.at[s], ag_recv.at[k], (p + 1, v))

    def send_left(k, s):
        return remote(vb.at[k], vb.at[k], ag_send.at[3 + s], ag_recv.at[k], (p - 1, v))

    def wait_views(k):
        remote(vb.at[k], vb.at[k], ag_send.at[0], ag_recv.at[k], (p, v)).wait_recv()

    @pl.when(p < NPB - 1)
    def _():
        send_right(p, 0).start()

    @pl.when(p > 0)
    def _():
        send_left(p, 0).start()

    def forward(k):
        @pl.when(jnp.logical_and(k < p, p < NPB - 1))
        def _():
            send_right(k, p - k).start()

        @pl.when(jnp.logical_and(k > p, p > 0))
        def _():
            send_left(k, k - p).start()

    side = p // 2
    near = p + side * (3 - 2 * p)
    base = [near, 1 - near, 2, 3]
    order = [b + side * (3 - 2 * b) for b in base]

    k0, k1, k2 = kscale_ref[0], kscale_ref[1], kscale_ref[2]

    def scale_of(k):
        kind = kind_ref[k]
        return jnp.where(kind == 0, k0, jnp.where(kind == 1, k1, k2))

    def cast_queries(r, carry):
        pltpu.make_async_copy(q_hbm.at[pl.ds(r * gpc, gpc)], gq.at[pl.ds(r * gpc, gpc)], qsem.at[r]).wait()
        block = gq[pl.ds(r * gpc, gpc)].reshape(CHUNK, width)
        at = pl.multiple_of(r * CHUNK, CHUNK)
        qb[pl.ds(at, CHUNK), :] = block.astype(BF16)
        qt[:, pl.ds(at, CHUNK)] = block.T.astype(BF16)
        return carry

    lax.fori_loop(0, nchunk, cast_queries, 0)

    def spread(r, carry):
        at = pl.multiple_of(r * 128, 128)
        qwrep[pl.ds(at, 128), :] = jnp.broadcast_to(qw_ref[pl.ds(r, 1), :], (128, 128)).T
        posrep[pl.ds(at, 128), :] = jnp.broadcast_to(pos_ref[pl.ds(r, 1), :], (128, 128)).T
        return carry

    lax.fori_loop(0, rows // 128, spread, 0)

    lane = lax.broadcasted_iota(jnp.int32, (CHUNK, 128), 1)

    def first_pass(t):
        k = order[t]
        scale = scale_of(k) * LOG2E

        def step(r, carry):
            peak, total = carry
            at = pl.multiple_of(r * CHUNK, CHUNK)
            s = lax.dot_general(qb[pl.ds(at, CHUNK), :], vb[k], (((1,), (1,)), ((), ())),
                                preferred_element_type=F32) * scale
            S[k, pl.ds(at, CHUNK), :] = s
            m = jnp.max(s, axis=1, keepdims=True)
            lse = m + jnp.log2(jnp.sum(jnp.exp2(s - m), axis=1, keepdims=True))
            if t == 0:
                stat[pl.ds(at, CHUNK), :] = jnp.broadcast_to(lse, (CHUNK, 128))
            else:
                stat[pl.ds(at, CHUNK), :] = jnp.where(lane == t, lse, stat[pl.ds(at, CHUNK), :])
            merged = jnp.maximum(peak, jnp.max(s, axis=0, keepdims=True))
            total = total * jnp.exp2(peak - merged) + jnp.sum(jnp.exp2(s - merged), axis=0, keepdims=True)
            return merged, total

        start = (jnp.full((1, vcols), -jnp.inf, F32), jnp.zeros((1, vcols), F32))
        peak, total = lax.fori_loop(0, nchunk, step, start)
        colst[p, k] = peak + jnp.log2(total)

    first_pass(0)
    for t in (1, 2):
        wait_views(order[t])
        forward(order[t])
    first_pass(1)
    first_pass(2)
    wait_views(order[3])
    forward(order[3])
    first_pass(3)

    sends = []

    def go(copy):
        copy.start()
        sends.append(copy)

    for d in range(1, NPB):
        go(remote(colst.at[p], colst.at[p], col_send.at[d], col_recv.at[p], ((p + d) % NPB, v)))

    def gather_rows(r, carry):
        at = pl.multiple_of(r * 128, 128)
        turned = stat[pl.ds(at, 128), :].T[0:NPB, :]
        m = jnp.max(turned, axis=0, keepdims=True)
        rowa[a_me, pl.ds(r, 1), :] = m + jnp.log2(jnp.sum(jnp.exp2(turned - m), axis=0, keepdims=True))
        return carry

    lax.fori_loop(0, rows // 128, gather_rows, 0)

    def log_sum(parts):
        m = parts[0]
        for part in parts[1:]:
            m = jnp.maximum(m, part)
        total = jnp.exp2(parts[0] - m)
        for part in parts[1:]:
            total = total + jnp.exp2(part - m)
        return m + jnp.log2(total)

    def exchange_a(buf, ssem, rsem, base_):
        for d in range(1, NA):
            go(remote(buf.at[a_me], buf.at[a_me], ssem.at[base_ + d], rsem.at[base_ + a_me], peers_a[d - 1]))

    def exchange_b(buf, ssem, rsem, base_):
        for d in range(1, NB):
            go(remote(buf.at[b_me], buf.at[b_me], ssem.at[base_ + d], rsem.at[base_ + b_me], peers_b[d - 1]))

    def collect(buf, ssem, rsem, base_, me, n):
        for d in range(1, n):
            src = (me + d) % n
            remote(buf.at[src], buf.at[src], ssem.at[base_ + d], rsem.at[base_ + src], (p, v)).wait_recv()

    exchange_a(rowa, row_send, row_recv, 0)
    collect(rowa, row_send, row_recv, 0, a_me, NA)
    rowb[b_me] = log_sum([rowa[i] for i in range(NA)])
    exchange_b(rowb, row_send, row_recv, NA)
    collect(colst, col_send, col_recv, 0, p, NPB)
    col_lse = [log_sum([colst[i, k] for i in range(NPB)]) for k in range(NPB)]
    for k in range(NPB):
        colfin[k] = col_lse[k] - jnp.log2(vw_ref[k])
    collect(rowb, row_send, row_recv, NA, b_me, NB)
    rowfin[...] = log_sum([rowb[i] for i in range(NB)]) - jnp.log2(qw_ref[...])

    def spread_lse(r, carry):
        at = pl.multiple_of(r * 128, 128)
        arep[pl.ds(at, 128), :] = jnp.broadcast_to(rowfin[pl.ds(r, 1), :], (128, 128)).T
        return carry

    lax.fori_loop(0, rows // 128, spread_lse, 0)

    lane_f = lax.broadcasted_iota(jnp.int32, (CHUNK, 128), 1).astype(F32)
    row_id = lax.broadcasted_iota(jnp.int32, (CHUNK, 128), 0)

    def second_pass(t):
        k = order[t]
        scale = scale_of(k)
        shift = colfin[k]
        weight = vw_ref[k]
        owner = own_ref[k] - p * rows

        def step(r, carry):
            at = pl.multiple_of(r * CHUNK, CHUNK)
            ra, rw, rp = arep[pl.ds(at, CHUNK), :], qwrep[pl.ds(at, CHUNK), :], posrep[pl.ds(at, CHUNK), :]
            out = []
            for h in range(vcols // 128):
                part = slice(h * 128, (h + 1) * 128)
                s = S[k, pl.ds(at, CHUNK), part]
                g = jnp.exp2(s - ra) + jnp.exp2(s - shift[:, part])
                col = lane_f + (k * vcols + h * 128).astype(F32)
                g = g - jnp.where(rp == col, rw, 0.0)
                g = g - jnp.where(row_id == owner[:, part] - at, weight[:, part], 0.0)
                H[k, pl.ds(at, CHUNK), part] = (g * scale[:, part]).astype(BF16)
                out.append(carry[h] + jnp.sum(g * s, axis=0, keepdims=True))
            return tuple(out)

        zero = jnp.zeros((1, 128), F32)
        terms = lax.fori_loop(0, nchunk, step, (zero,) * (vcols // 128))
        kind = kind_ref[k]
        kinds = []
        for t_ in range(3):
            kinds.append(sum(jnp.where(kind[:, h * 128:(h + 1) * 128] == t_, terms[h], 0.0)
                             for h in range(vcols // 128)))

        def grad_views(i, carry):
            at = pl.multiple_of(i * CHUNK, CHUNK)
            gvt[k, pl.ds(at, CHUNK), :] = jnp.dot(qt[pl.ds(at, CHUNK), :], H[k], preferred_element_type=F32)
            return carry

        lax.fori_loop(0, width // CHUNK, grad_views, 0)
        return kinds

    def right(k):
        return remote(zs.at[k], zrl.at[k], z_send.at[k], zl_recv.at[k], (p + 1, v))

    def left(k):
        return remote(zs.at[k], zrr.at[k], z_send.at[k], zr_recv.at[k], (p - 1, v))

    kinds = [jnp.zeros((1, 128), F32)] * 3
    for t in (3, 2, 1, 0):
        more = second_pass(t)
        kinds = [a + b for a, b in zip(kinds, more)]
        if t > 0:
            k = order[t]

            @pl.when(p == 0)
            def _():
                zs[k] = gvt[k].astype(BF16)
                right(k).start()

            @pl.when(p == NPB - 1)
            def _():
                zs[k] = gvt[k].astype(BF16)
                left(k).start()

    ta[a_me] = jnp.concatenate(kinds + [jnp.zeros((5, 128), F32)], axis=0) * (LN2 / total_queries)
    exchange_a(ta, t_send, t_recv, 0)

    def relay_right(k):
        right(k).wait_recv()
        zs[k] = (gvt[k] + zrl[k].astype(F32)).astype(BF16)
        right(k).start()

    def relay_left(k):
        left(k).wait_recv()
        zs[k] = (gvt[k] + zrr[k].astype(F32)).astype(BF16)
        left(k).start()

    @pl.when(p == 1)
    def _():
        relay_right(3)

    @pl.when(p == 2)
    def _():
        relay_left(0)

    other = vert_of(zh, y, x, 1 - core)

    def core_copy(r):
        return remote(gq.at[pl.ds(r * gpc, gpc), 1 - core], crecv.at[pl.ds(r * gpc, gpc)],
                      c_send.at[r], c_recv.at[r], (p, other))

    def grad_queries(r, carry):
        at = pl.multiple_of(r * CHUNK, CHUNK)
        acc = jnp.dot(H[0, pl.ds(at, CHUNK), :], vb[0], preferred_element_type=F32)
        for k in range(1, NPB):
            acc = acc + jnp.dot(H[k, pl.ds(at, CHUNK), :], vb[k], preferred_element_type=F32)
        gq[pl.ds(r * gpc, gpc)] = acc.reshape(gpc, 2, CHUNK // (2 * gpc), width)
        core_copy(r).start()
        return carry

    lax.fori_loop(0, nchunk, grad_queries, 0)

    half = width // 2
    for r in range(nchunk):
        core_copy(r).wait_recv()
        for g in range(r * gpc, (r + 1) * gpc):
            gz, gy, gx = g // (NX * NY), (g // NX) % NY, g % NX
            val = gq[g, core] + crecv[g]
            crecv[g] = val
            sa1[gx, gz * NY + gy] = val[:, :half].astype(BF16)
            sb1[gy, gz * NX + gx] = val[:, half:].astype(BF16)

    def to_x(src, dst, at, d):
        return remote(src, dst, x_send.at[at + d], x_recv.at[at + x], (p, vert_of(zh, y, (x + d) % NX, core)))

    def to_y(src, dst, at, d):
        return remote(src, dst, x_send.at[at + d], x_recv.at[at + y], (p, vert_of(zh, (y + d) % NY, x, core)))

    for d in range(1, 4):
        go(to_x(sa1.at[(x + d) % NX], ra1.at[x], 0, d))
        go(to_y(sb1.at[(y + d) % NY], rb1.at[y], 4, d))

    collect(ta, t_send, t_recv, 0, a_me, NA)
    tb[b_me] = sum(ta[i] for i in range(NA))
    exchange_b(tb, t_send, t_recv, NA)

    @pl.when(p == 1)
    def _():
        relay_right(2)
        relay_left(0)

    @pl.when(p == 2)
    def _():
        relay_left(1)
        relay_right(3)

    collect(tb, t_send, t_recv, NA, b_me, NB)
    tp[p] = sum(tb[i] for i in range(NB))
    for d in range(1, NPB):
        go(remote(tp.at[p], tp.at[p], t_send.at[NA + NB + d], t_recv.at[NA + NB + p], ((p + d) % NPB, v)))

    collect(ra1, x_send, x_recv, 0, x, NX)
    for gz in range(2):
        for gy in range(NY):
            i = gz * NY + gy
            val = crecv[i * NX + x][:, :half]
            for d in range(1, NX):
                val = val + ra1[(x + d) % NX, i].astype(F32)
            acca[i] = val
            sa2[gy, gz] = val.astype(BF16)
    for d in range(1, 4):
        go(to_y(sa2.at[(y + d) % NY], ra2.at[y], 8, d))

    collect(rb1, x_send, x_recv, 4, y, NY)
    for gz in range(2):
        for gx in range(NX):
            i = gz * NX + gx
            val = crecv[gz * (NX * NY) + y * NX + gx][:, half:]
            for d in range(1, NY):
                val = val + rb1[(y + d) % NY, i].astype(F32)
            accb[i] = val
            sb2[gx, gz] = val.astype(BF16)
    for d in range(1, 4):
        go(to_x(sb2.at[(x + d) % NX], rb2.at[x], 12, d))

    collect(ra2, x_send, x_recv, 8, y, NY)
    for gz in range(2):
        val = acca[gz * NY + y]
        for d in range(1, NY):
            val = val + ra2[(y + d) % NY, gz].astype(F32)
        acca[gz * NY + y] = val
    far = (p, vert_of(1 - zh, y, x, core))
    last_a = remote(acca.at[(1 - zh) * NY + y], zra, x_send.at[16], x_recv.at[16], far)
    last_a.start()

    collect(rb2, x_send, x_recv, 12, x, NX)
    for gz in range(2):
        val = accb[gz * NX + x]
        for d in range(1, NX):
            val = val + rb2[(x + d) % NX, gz].astype(F32)
        accb[gz * NX + x] = val
    last_b = remote(accb.at[(1 - zh) * NX + x], zrb, x_send.at[17], x_recv.at[17], far)
    last_b.start()

    for d in range(1, NPB):
        src = (p + d) % NPB
        remote(tp.at[src], tp.at[src], t_send.at[0], t_recv.at[NA + NB + src], (p, v)).wait_recv()
    sums = sum(tp[i] for i in range(NPB))
    tg_out[...] = jnp.broadcast_to(jnp.sum(sums, axis=1, keepdims=True), sums.shape)

    last_a.wait_recv()
    gq_out[:, :half] = acca[zh * NY + y] + zra[...]
    last_b.wait_recv()
    gq_out[:, half:] = accb[zh * NX + x] + zrb[...]

    @pl.when(p > 0)
    def _():
        right(p).wait_recv()
        gvt[p] = gvt[p] + zrl[p].astype(F32)

    @pl.when(p < NPB - 1)
    def _():
        left(p).wait_recv()
        gvt[p] = gvt[p] + zrr[p].astype(F32)

    gv_out[...] = gvt[p].T

    last_a.wait_send()
    last_b.wait_send()
    for copy in sends:
        copy.wait_send()
    for r in range(nchunk):
        core_copy(r).wait_send()
    for k in range(NPB):
        @pl.when(k != p)
        def _():
            right(k).wait_send()
    for s in range(NPB - 1):
        @pl.when(jnp.logical_and(p < NPB - 1, s <= p))
        def _():
            send_right(p, s).wait_send()

        @pl.when(jnp.logical_and(p > 0, s <= NPB - 1 - p))
        def _():
            send_left(p, s).wait_send()


def on_device(queries, views, positives, query_weight, owners, view_weight, view_kinds, kind_scale):
    rows, width = queries.shape
    vcols = views.shape[0]
    tile_cols = NPB * vcols
    nchunk = rows // CHUNK
    groups = 4 * nchunk
    sub = rows // (2 * groups)
    half = width // 2
    col_anchor = lax.axis_index("vert") * tile_cols
    pos = (positives - col_anchor).astype(F32).reshape(rows // 128, 128)
    qw = query_weight.reshape(rows // 128, 128)
    own = owners.reshape(NPB, 1, vcols)
    vw = view_weight.reshape(NPB, 1, vcols)
    kind = view_kinds.reshape(NPB, 1, vcols)
    vmem = pl.BlockSpec(memory_space=pltpu.VMEM)
    V = pltpu.VMEM
    dma = pltpu.SemaphoreType.DMA
    gq, gv, tg = pl.pallas_call(
        functools.partial(kernel, rows * NPB),
        out_shape=(
            jax.ShapeDtypeStruct((sub, width), F32),
            jax.ShapeDtypeStruct((vcols, width), F32),
            jax.ShapeDtypeStruct((8, 128), F32),
        ),
        in_specs=[pl.BlockSpec(memory_space=pltpu.SMEM), vmem, pl.BlockSpec(memory_space=pl.ANY)] + [vmem] * 5,
        out_specs=(vmem, vmem, vmem),
        scratch_shapes=[
            V((rows, width), BF16),
            V((width, rows), BF16),
            V((NPB, vcols, width), BF16),
            V((NPB, rows, vcols), F32),
            V((NPB, rows, vcols), BF16),
            V((rows, 128), F32),
            V((rows, 128), F32),
            V((rows, 128), F32),
            V((rows, 128), F32),
            V((groups, 2, sub, width), F32),
            V((NPB, width, vcols), F32),
            V((NPB, width, vcols), BF16),
            V((NPB, width, vcols), BF16),
            V((NPB, width, vcols), BF16),
            V((groups, sub, width), F32),
            V((NX, 8, sub, half), BF16),
            V((NY, 8, sub, half), BF16),
            V((NX, 8, sub, half), BF16),
            V((NY, 8, sub, half), BF16),
            V((NY, 2, sub, half), BF16),
            V((NX, 2, sub, half), BF16),
            V((NY, 2, sub, half), BF16),
            V((NX, 2, sub, half), BF16),
            V((8, sub, half), F32),
            V((8, sub, half), F32),
            V((sub, half), F32),
            V((sub, half), F32),
            V((NPB, NPB, 1, vcols), F32),
            V((NA, rows // 128, 128), F32),
            V((NB, rows // 128, 128), F32),
            V((NPB, 1, vcols), F32),
            V((rows // 128, 128), F32),
            V((NA, 8, 128), F32),
            V((NB, 8, 128), F32),
            V((NPB, 8, 128), F32),
            dma((nchunk,)),
            dma((6,)), dma((NPB,)),
            dma((NPB,)), dma((NPB,)),
            dma((NA + NB,)), dma((NA + NB,)),
            dma((NA + NB + NPB,)), dma((NA + NB + NPB,)),
            dma((nchunk,)), dma((nchunk,)),
            dma((18,)), dma((18,)),
            dma((NPB,)), dma((NPB,)), dma((NPB,)),
        ],
        compiler_params=pltpu.CompilerParams(collective_id=0, has_side_effects=True,
                                             vmem_limit_bytes=62 * 1024 * 1024),
    )(kind_scale, views, queries.reshape(groups, 2, sub, width), pos, qw, own, vw, kind)
    return gq, gv, tg[:3, 0]


def solution(mesh):
    in_specs = (P("pb", None), P(("vert", "pb"), None), P("pb"), P("pb"), P("vert"), P("vert"), P("vert"), P())
    out_specs = (P(("pb", "vert"), None), P(("vert", "pb"), None), P())
    return jax.shard_map(on_device, mesh=mesh, in_specs=in_specs, out_specs=out_specs, check_vma=False)
```

time: 798 us -> 110 us (0.14)
  blocking collectives: 507 us -> 0 us
  waiting for transfers between devices: 201 us -> 0 us
  Pallas kernels: 0 us -> 102 us
  other arithmetic: 38.4 us -> 1.3 us
  matrix products: 26.8 us -> 0 us
  between operations: 14 us -> 0.64 us
    psum x3 -> x0, blocking collectives: 299 us -> none  [the longest x1 203 us: on_device(): row_sum = lax.psum(row_total * jnp.exp(row_peak - row_max), 'vert')]
    pmax x2 -> x0, blocking collectives: 208 us -> none  [the longest x1 198 us: on_device(): row_max = lax.pmax(row_peak, 'vert')]
    reduce_scatter x2 -> x0, waiting for transfers between devices: 160 us -> none  [the longest x1 160 us: on_device(): lax.psum_scatter(jnp.dot(half_tile, v_half, preferred_element_type=jnp.fl...]
    pallas_call x0 -> x1, Pallas kernels: none -> 102 us  [on_device(): pl.pallas_call(functools.partial(kernel, rows * NPB), out_shape=(jax.Shap...]
    all_gather x1 -> x0, waiting for transfers between devices: 40.8 us -> none  [on_device(): lax.all_gather(views.astype(jnp.bfloat16), 'pb', axis=0, tiled=True)]
    dot_general x6 -> x0, matrix products: 26.8 us -> none  [the longest x4 11 us: scored(): lax.dot_general(q_block, v_half, (((1,), (1,)), ((), ())), preferred_elem...]
    dynamic_update_slice x4 -> x0, other arithmetic: 14.6 us -> none  [on_device(): lax.scan(second_pass, jnp.zeros((tile_cols,), jnp.float32), operands)]
    reduce_sum x10 -> x0, other arithmetic: 13.6 us -> none  [the longest x4 10.5 us: second_pass(): col_terms = col_terms + jnp.sum(grad * scores, axis=0)]
  transfers between devices with their start and end apart: 3 -> 0, of which waited for: 2 -> 0; matrix products, arithmetic and copies ran while one was open for 2% -> 0% of each run, Pallas kernels for 0% -> 0%
where the time goes in v1:
time: 110 us; the launch traced here: 109 us
  Pallas kernels  102 us (93%)
  local copies, waits for them, and re-layouts  4.91 us (4%)
  other arithmetic  1.3 us (1%)
    pallas_call x1, Pallas kernels, on_device(): pl.pallas_call(functools.partial(kernel, rows * NPB), out_shape=(jax.Shap...  102 us
    unnamed x2, local copies, waits for them, and re-layouts  3.6 us

profile of v1, /device:TPU:2, one launch (start us, length us, event | category | flops | bytes accessed | tf_op | source)
XLA Modules:
  0.0 108.8 jit_solution(5738073373242086051)
XLA Ops:
  0.6 1.3 %convert_bitcast_fusion.pos_ref = f32[16,128]{1,0:T(8,128)} fusion(s32[2048]{0:T(1024)} %param.10, s32[]{:T(128)S(6)} %mul.3), kind=kLoop, calls=%fused_computation | loop fusion | flops 4096 | bytes 16388 | tf_op jit(solution)/shard_map/reshape | solution.py:449
  1.9 101.9 %shard_map.103 = (f32[32,768]{1,0:T(8,128)}, f32[256,768]{1,0:T(8,128)}, f32[8,128]{1,0:T(8,128)}) custom-call(f32[3]{0:T(128)} %kscale_ref.1, f32[256,768]{1,0:T(8,128)} %views_ref.1, f32[32,2,32,768]{3,2,1,0:T(8,128)} %bitcast.7, f32[16,128]{1,0:T(8,128)} %convert_bitcast_fusion.pos_ref, f32[16,128]{1,0:T(8,128)} %bitcast.8, s32[4,1,256]{2,1,0:T(1,128)} %bitcast.9, ...), custom_call_target="tpu_custom_call" | custom-call | tf_op jit(solution)/shard_map/pallas_call | solution.py:457
  103.9 1.3 %slice_reduce_fusion = f32[3]{0:T(128)} fusion(f32[8,128]{1,0:T(8,128)} %get-tuple-element.8), kind=kLoop, calls=%fused_computation.1 | loop fusion | bytes 24 | tf_op jit(solution)/shard_map/slice | solution.py:514
  105.2 1.5 %copy.13 = f32[32,768]{1,0:T(8,128)} copy(f32[32,768]{1,0:T(8,128)} %get-tuple-element.12) | data formatting | bytes 196608
  106.7 2.1 %copy.14 = f32[256,768]{1,0:T(8,128)} copy(f32[256,768]{1,0:T(8,128)} %get-tuple-element.13) | data formatting | bytes 1572864

commit v2 on v0

v2 whole, which is shorter than its diff:
```python
import functools
import math

import jax
import jax.numpy as jnp
from jax import lax
from jax.experimental import pallas as pl
from jax.experimental.pallas import tpu as pltpu
from jax.sharding import PartitionSpec as P

MESH = pl.DeviceIdType.MESH
LOG2E = math.log2(math.e)
LN2 = math.log(2.0)
NPB = 4
NX = 4
NY = 4
NA = 8
NB = 16
CHUNK = 256
F32 = jnp.float32
BF16 = jnp.bfloat16


def kernel(total_queries, kscale_ref, views_ref, q_hbm, pos_ref, qw_ref, own_ref, vw_ref, kind_ref,
           gq_out, gv_out, tg_out,
           qb, qt, qf, vb, S, H, qslice, qzs, pq, pqf, rep, qwrep, posrep, gown, csend, crecv,
           sa1, sb1, ra1, rb1, sa2, sb2, ra2, rb2, acca, accb, res, zres, gvt, zs, zr,
           colpart, rowpart, colx, colfin, rowa, rowb, rowfin, ta, tb, tp,
           qsem, slsem, ag_send, ag_recv, core_send, core_recv, vz_send, vz_recv,
           col_send, col_recv, row_send, row_recv, t_send, t_recv,
           c_send, c_recv, x_send, x_recv, z_send, z_recv):
    p = lax.axis_index("pb")
    v = lax.axis_index("vert")
    core = v % 2
    x = (v // 2) % NX
    y = (v // (2 * NX)) % NY
    zh = v // (2 * NX * NY)
    even = p % 2
    upper = p // 2
    mate = p + 1 - 2 * even
    far = (p + 2) % NPB
    a_me = v % NA
    b_me = (upper * 2 + zh) * NY + y
    rows, width = qb.shape
    nchunk = rows // CHUNK
    vcols = views_ref.shape[0]
    half = width // 2
    sub = gown.shape[3]

    def vert_of(zh_, y_, x_, c_):
        return ((zh_ * NY + y_) * NX + x_) * 2 + c_

    def remote(src, dst, ssem, rsem, dev):
        return pltpu.make_async_remote_copy(src_ref=src, dst_ref=dst, send_sem=ssem, recv_sem=rsem,
                                            device_id=dev, device_id_type=MESH)

    here = (p, v)
    sends = []

    def go(copy):
        copy.start()
        sends.append(copy)

    sl_a = (y * NX + x) * 2 + core
    sl_b = 8 * NY + (x * NY + y) * 2 + core
    slices = []
    for i, sl in enumerate((sl_a, sl_b)):
        slices.append(pltpu.make_async_copy(q_hbm.at[sl // 16, (sl // 4) % 4, sl % 4], qslice.at[i], slsem.at[i]))
        slices[-1].start()

    def load(r):
        part = (r // 2, pl.ds((r % 2) * 2, 2))
        return pltpu.make_async_copy(q_hbm.at[part], gown.at[part], qsem.at[r])

    for r in range(nchunk):
        load(r).start()

    peers_a = [(p, (v // NA) * NA + (a_me + d) % NA) for d in range(1, NA)]
    peers_b = []
    for d in range(1, NB):
        i = (b_me + d) % NB
        peers_b.append(((i // 8) * 2 + even, vert_of((i // NY) % 2, i % NY, x, core)))
    peers = peers_a + peers_b + [(mate, v)]
    barrier = pltpu.get_barrier_semaphore()
    for dev in peers:
        pl.semaphore_signal(barrier, inc=1, device_id=dev, device_id_type=MESH)
    vb[0:vcols, :] = views_ref[...].astype(BF16)
    nrow = rows // 128
    pq[0:nrow, :] = pos_ref[...].astype(F32)
    pq[nrow:2 * nrow, :] = qw_ref[...]
    for i in range(2):
        slices[i].wait()
        qzs[i] = qslice[i].astype(BF16)
    pl.semaphore_wait(barrier, len(peers))

    def to_far(i, src, dst):
        return remote(src, dst, vz_send.at[i], vz_recv.at[i], (far, v))

    go(to_far(0, qzs.at[0], qf.at[0, y, x, core]))
    go(to_far(1, qzs.at[1], qf.at[1, x, y, core]))
    views_copy = remote(vb.at[pl.ds(0, vcols)], vb.at[pl.ds(vcols, vcols)], vz_send.at[2], vz_recv.at[2], (mate, v))
    go(views_copy)
    go(to_far(3, pq, pqf))

    def to_x(d):
        return (p, vert_of(zh, y, (x + d) % NX, core))

    def to_y(d):
        return (p, vert_of(zh, (y + d) % NY, x, core))

    twin = (p, vert_of(zh, y, x, 1 - core))

    k0, k1, k2 = kscale_ref[0], kscale_ref[1], kscale_ref[2]
    blocks = (p, mate)

    def scale_of(k):
        kind = kind_ref[k]
        return jnp.where(kind == 0, k0, jnp.where(kind == 1, k1, k2))

    scales = [scale_of(k) for k in blocks]
    scales2 = [s * LOG2E for s in scales]

    def cast_queries(r, carry):
        load(r).wait()
        block = gown[r // 2, pl.ds((r % 2) * 2, 2)].reshape(CHUNK, width)
        at = pl.multiple_of(r * CHUNK, CHUNK)
        qb[pl.ds(at, CHUNK), :] = block.astype(BF16)
        qt[:, pl.ds(at, CHUNK)] = block.T.astype(BF16)
        return carry

    lax.fori_loop(0, nchunk, cast_queries, 0)

    def score(q, at, ch, slots, row_at):
        tiles = []
        for sl in slots:
            cols = slice(sl * vcols, (sl + 1) * vcols)
            s = lax.dot_general(q, vb[cols, :], (((1,), (1,)), ((), ())),
                                preferred_element_type=F32) * scales2[sl]
            S[pl.ds(at, CHUNK), cols] = s
            peak = jnp.max(s, axis=0, keepdims=True)
            colpart[sl, pl.ds(ch, 1), :] = peak + jnp.log2(jnp.sum(jnp.exp2(s - peak), axis=0, keepdims=True))
            tiles += [s[:, h * 128:(h + 1) * 128] for h in range(vcols // 128)]
        m = functools.reduce(jnp.maximum, tiles)
        total = functools.reduce(jnp.add, [jnp.exp2(t - m) for t in tiles])
        for i in range(CHUNK // 128):
            mt = m[i * 128:(i + 1) * 128, :].T
            lt = total[i * 128:(i + 1) * 128, :].T
            peak = jnp.max(mt, axis=0, keepdims=True)
            lse = peak + jnp.log2(jnp.sum(lt * jnp.exp2(mt - peak), axis=0, keepdims=True))
            rowpart[row_at[0], pl.ds(row_at[1] * 2 + i, 1), :] = lse

    def own_pass(sl, first, last):
        def step(i, carry):
            for j in range(2):
                r = i * 2 + j
                at = pl.multiple_of(r * CHUNK, CHUNK)
                score(qb[pl.ds(at, CHUNK), :], at, r, (sl,), (sl, r))
            return carry

        lax.fori_loop(first // 2, last // 2, step, 0)

    def far_pass(parts):
        for h, o in parts:
            r = h * 4 + o
            q = qf[h, o].reshape(CHUNK, width)
            at = pl.multiple_of(rows + r * CHUNK, CHUNK)
            score(q, at, r + nchunk, (0, 1), (2, r))
            qt[:, pl.ds(at, CHUNK)] = q.T

    def got(ref, sem):
        remote(ref, ref, sem, sem, here).wait_recv()

    got(qf.at[0, y, x, core], vz_recv.at[0])
    for d in (1, 3, 2):
        go(remote(qf.at[0, y, x, core], qf.at[0, y, x, core], ag_send.at[d], ag_recv.at[x], to_x(d)))
    got(qf.at[1, x, y, core], vz_recv.at[1])
    for d in (1, 3, 2):
        go(remote(qf.at[1, x, y, core], qf.at[1, x, y, core], ag_send.at[4 + d], ag_recv.at[4 + y], to_y(d)))

    own_pass(0, 0, 4)

    for d in (1, 3, 2):
        got(qf.at[0, y, (x + d) % NX, core], ag_recv.at[(x + d) % NX])
    for d in (1, 3, 2):
        go(remote(qf.at[0, y, :, core], qf.at[0, y, :, core], ag_send.at[8 + d], ag_recv.at[8 + y], to_y(d)))
    for d in (1, 3, 2):
        got(qf.at[1, x, (y + d) % NY, core], ag_recv.at[4 + (y + d) % NY])
    for d in (1, 3, 2):
        go(remote(qf.at[1, x, :, core], qf.at[1, x, :, core], ag_send.at[12 + d], ag_recv.at[12 + x], to_x(d)))

    def to_twin(h, o):
        part = qf.at[h, o, :, core]
        go(remote(part, part, core_send.at[h * 4 + o], core_recv.at[h * 4 + o], twin))

    def from_twin(h, o):
        got(qf.at[h, o, :, 1 - core], core_recv.at[h * 4 + o])

    to_twin(0, y)
    to_twin(1, x)

    own_pass(0, 4, 8)

    def spread(src, first, dst, at0):
        def step(r, carry):
            at = pl.multiple_of(at0 + r * 128, 128)
            dst[pl.ds(at, 128), :] = jnp.broadcast_to(src[pl.ds(first + r, 1), :], (128, 128)).T
            return carry

        lax.fori_loop(0, nrow, step, 0)

    spread(pq, 0, posrep, 0)
    spread(pq, nrow, qwrep, 0)
    got(vb.at[pl.ds(vcols, vcols)], vz_recv.at[2])
    own_pass(1, 0, 8)
    got(pqf, vz_recv.at[3])
    spread(pqf, 0, posrep, rows)
    spread(pqf, nrow, qwrep, rows)

    from_twin(0, y)
    from_twin(1, x)
    far_pass([(0, y), (1, x)])
    for d in (1, 3):
        got(qf.at[0, (y + d) % NY, :, core], ag_recv.at[8 + (y + d) % NY])
        to_twin(0, (y + d) % NY)
        got(qf.at[1, (x + d) % NX, :, core], ag_recv.at[12 + (x + d) % NX])
        to_twin(1, (x + d) % NX)
    for d in (1, 3):
        from_twin(0, (y + d) % NY)
        from_twin(1, (x + d) % NX)
        far_pass([(0, (y + d) % NY), (1, (x + d) % NX)])
    got(qf.at[0, (y + 2) % NY, :, core], ag_recv.at[8 + (y + 2) % NY])
    to_twin(0, (y + 2) % NY)
    got(qf.at[1, (x + 2) % NX, :, core], ag_recv.at[12 + (x + 2) % NX])
    to_twin(1, (x + 2) % NX)
    from_twin(0, (y + 2) % NY)
    from_twin(1, (x + 2) % NX)
    far_pass([(0, (y + 2) % NY), (1, (x + 2) % NX)])

    def log_sum(parts):
        m = functools.reduce(jnp.maximum, parts)
        return m + jnp.log2(functools.reduce(jnp.add, [jnp.exp2(t - m) for t in parts]))

    def exchange_a(buf, ssem, rsem, base):
        for d in range(1, NA):
            go(remote(buf.at[a_me], buf.at[a_me], ssem.at[base + d], rsem.at[base + a_me], peers_a[d - 1]))

    def exchange_b(buf, ssem, rsem, base):
        for d in range(1, NB):
            go(remote(buf.at[b_me], buf.at[b_me], ssem.at[base + d], rsem.at[base + b_me], peers_b[d - 1]))

    def collect(buf, rsem, base, me, n):
        for d in range(1, n):
            src = (me + d) % n
            got(buf.at[src], rsem.at[base + src])

    rowa[a_me, upper] = log_sum([rowpart[0], rowpart[1]])
    rowa[a_me, 1 - upper] = rowpart[2]
    exchange_a(rowa, row_send, row_recv, 0)
    for sl in range(2):
        part = colpart[sl]
        m = jnp.max(part, axis=0, keepdims=True)
        at = even if sl == 0 else 1 - even
        colx[even, at] = m + jnp.log2(jnp.sum(jnp.exp2(part - m), axis=0, keepdims=True))
    go(remote(colx.at[even], colx.at[even], col_send.at[0], col_recv.at[0], (mate, v)))
    collect(rowa, row_recv, 0, a_me, NA)
    rowb[b_me] = log_sum([rowa[i] for i in range(NA)])
    exchange_b(rowb, row_send, row_recv, NA)
    got(colx.at[1 - even], col_recv.at[0])
    for sl in range(2):
        at = even if sl == 0 else 1 - even
        colfin[sl] = log_sum([colx[0, at], colx[1, at]]) - jnp.log2(vw_ref[blocks[sl]])
    collect(rowb, row_recv, NA, b_me, NB)
    row_lse = log_sum([rowb[i] for i in range(NB)])
    rowfin[...] = row_lse
    pqw = (pq, pqf)
    for b in range(2):
        at = upper if b == 0 else 1 - upper
        rowpart[b] = rowfin[at] - jnp.log2(pqw[b][nrow:2 * nrow, :])

    def spread_lse(b):
        def step(i, carry):
            for j in range(2):
                r = i * 2 + j
                at = pl.multiple_of(b * rows + r * 128, 128)
                rep[pl.ds(at, 128), :] = jnp.broadcast_to(rowpart[b, pl.ds(r, 1), :], (128, 128)).T
            return carry

        lax.fori_loop(0, nrow // 2, step, 0)

    spread_lse(1)

    lane = lax.broadcasted_iota(jnp.int32, (CHUNK, 128), 1).astype(F32)
    row_id = lax.broadcasted_iota(jnp.int32, (CHUNK, 128), 0)
    ntile = 2 * vcols // 128
    per = vcols // 128

    def tile(arr, h):
        return arr[h // per][:, (h % per) * 128:(h % per + 1) * 128]

    weights = [vw_ref[k] for k in blocks]
    owners = [own_ref[k] for k in blocks]
    shifts = [colfin[0], colfin[1]]
    col0 = [(v * (NPB * vcols) + k * vcols).astype(F32) for k in blocks]
    rounds = [(1, 1 - zh), (1, zh), (0, 1 - zh), (0, zh)]

    def core_copy(rd, o):
        return remote(csend.at[rd, o], crecv.at[rd, o], c_send.at[rd * 4 + o], c_recv.at[rd * 4 + o], twin)

    def grad_step(rd, o, terms):
        b, z = rounds[rd]
        at = pl.multiple_of(b * rows + z * (rows // 2) + o * CHUNK, CHUNK)
        first_row = (p if b == 0 else far) * rows + z * (rows // 2) + o * CHUNK
        ra, rw, rp = rep[pl.ds(at, CHUNK), :], qwrep[pl.ds(at, CHUNK), :], posrep[pl.ds(at, CHUNK), :]
        out, pieces = [], []
        for h in range(ntile):
            s = S[pl.ds(at, CHUNK), h * 128:(h + 1) * 128]
            g = jnp.exp2(s - ra) + jnp.exp2(s - tile(shifts, h))
            col = lane + (col0[h // per] + (h % per) * 128)
            g = g - jnp.where(rp == col, rw, 0.0)
            g = g - jnp.where(row_id == tile(owners, h) - first_row, tile(weights, h), 0.0)
            pieces.append((g * tile(scales, h)).astype(BF16))
            out.append(terms[h] + jnp.sum(g * s, axis=0, keepdims=True))
        hh = jnp.concatenate(pieces, axis=1)
        H[pl.ds(at, CHUNK), :] = hh
        acc = jnp.dot(hh, vb[...], preferred_element_type=F32).reshape(NX, 2, sub, width)
        first, second = acc[:, 0], acc[:, 1]
        gown[rd, o] = jnp.where(core == 0, first, second)
        csend[rd, o] = jnp.where(core == 0, second, first).astype(BF16)
        core_copy(rd, o).start()
        return tuple(out)

    def grad_half(rd, part, terms):
        for j in range(2):
            terms = grad_step(rd, part * 2 + j, terms)
        return terms

    def fold_core(rd):
        def step(o, carry):
            core_copy(rd, o).wait_recv()
            for i in range(NX):
                val = gown[rd, o, i] + crecv[rd, o, i].astype(F32)
                gown[rd, o, i] = val
                sa1[rd, i, o] = val[:, :half].astype(BF16)
                sb1[rd, o, i] = val[:, half:].astype(BF16)
            return carry

        lax.fori_loop(0, NY, step, 0)
        for d in (1, 3, 2):
            go(remote(sa1.at[rd, (x + d) % NX], ra1.at[rd, x], x_send.at[rd * 16 + d], x_recv.at[rd * 16 + x], to_x(d)))
            go(remote(sb1.at[rd, (y + d) % NY], rb1.at[rd, y], x_send.at[rd * 16 + 4 + d], x_recv.at[rd * 16 + 4 + y],
                      to_y(d)))

    def fold_first(rd):
        for d in (1, 3, 2):
            got(ra1.at[rd, (x + d) % NX], x_recv.at[rd * 16 + (x + d) % NX])
        for o in range(NY):
            val = gown[rd, o, x][:, :half]
            for d in range(1, NX):
                val = val + ra1[rd, (x + d) % NX, o].astype(F32)
            acca[rd, o] = val
            sa2[rd, o] = val.astype(BF16)
        for d in (1, 3, 2):
            go(remote(sa2.at[rd, (y + d) % NY], ra2.at[rd, y], x_send.at[rd * 16 + 8 + d], x_recv.at[rd * 16 + 8 + y],
                      to_y(d)))
        for d in (1, 3, 2):
            got(rb1.at[rd, (y + d) % NY], x_recv.at[rd * 16 + 4 + (y + d) % NY])
        for i in range(NX):
            val = gown[rd, y, i][:, half:]
            for d in range(1, NY):
                val = val + rb1[rd, (y + d) % NY, i].astype(F32)
            accb[rd, i] = val
            sb2[rd, i] = val.astype(BF16)
        for d in (1, 3, 2):
            go(remote(sb2.at[rd, (x + d) % NX], rb2.at[rd, x], x_send.at[rd * 16 + 12 + d],
                      x_recv.at[rd * 16 + 12 + x], to_x(d)))

    def fold_second(rd):
        for d in (1, 3, 2):
            got(ra2.at[rd, (y + d) % NY], x_recv.at[rd * 16 + 8 + (y + d) % NY])
        val = acca[rd, y]
        for d in range(1, NY):
            val = val + ra2[rd, (y + d) % NY].astype(F32)
        res[rd, :, :half] = val
        for d in (1, 3, 2):
            got(rb2.at[rd, (x + d) % NX], x_recv.at[rd * 16 + 12 + (x + d) % NX])
        val = accb[rd, x]
        for d in range(1, NX):
            val = val + rb2[rd, (x + d) % NX].astype(F32)
        res[rd, :, half:] = val
        if rd < 3:
            b, z = rounds[rd]
            go(remote(res.at[rd], zres.at[rd], z_send.at[rd], z_recv.at[rd], (p if b == 0 else far, vert_of(z, y, x, core))))

    def grad_views(sl):
        def step(i, carry):
            at = pl.multiple_of(i * CHUNK, CHUNK)
            gvt[sl, pl.ds(at, CHUNK), :] = jnp.dot(qt[pl.ds(at, CHUNK), :], H[:, sl * vcols:(sl + 1) * vcols],
                                                   preferred_element_type=F32)
            return carry

        lax.fori_loop(0, width // CHUNK, step, 0)

    terms = (jnp.zeros((1, 128), F32),) * ntile
    terms = grad_half(0, 0, terms)
    terms = grad_half(0, 1, terms)
    spread_lse(0)
    fold_core(0)
    terms = grad_half(1, 0, terms)
    terms = grad_half(1, 1, terms)
    terms = grad_half(2, 0, terms)
    fold_core(1)
    terms = grad_half(2, 1, terms)
    fold_first(0)
    terms = grad_half(3, 0, terms)
    fold_core(2)
    terms = grad_half(3, 1, terms)
    grad_views(1)
    zs[...] = gvt[1].astype(BF16)
    go(remote(zs, zr, z_send.at[3], z_recv.at[3], (mate, v)))
    fold_core(3)

    kinds = []
    for t in range(3):
        kinds.append(functools.reduce(jnp.add, [
            jnp.where(tile([kind_ref[k] for k in blocks], h) == t, terms[h], 0.0) for h in range(ntile)]))
    ta[a_me] = jnp.concatenate(kinds + [jnp.zeros((5, 128), F32)], axis=0) * (LN2 / total_queries)
    exchange_a(ta, t_send, t_recv, 0)

    fold_first(1)
    grad_views(0)
    fold_second(0)
    collect(ta, t_recv, 0, a_me, NA)
    tb[b_me] = functools.reduce(jnp.add, [ta[i] for i in range(NA)])
    exchange_b(tb, t_send, t_recv, NA)
    fold_first(2)
    fold_second(1)
    collect(tb, t_recv, NA, b_me, NB)
    tp[even] = functools.reduce(jnp.add, [tb[i] for i in range(NB)])
    go(remote(tp.at[even], tp.at[even], t_send.at[NA + NB], t_recv.at[NA + NB], (mate, v)))
    fold_first(3)
    fold_second(2)
    got(zr, z_recv.at[3])
    gv_out[...] = (gvt[0] + zr[...].astype(F32)).T
    got(tp.at[1 - even], t_recv.at[NA + NB])
    sums = tp[0] + tp[1]
    tg_out[...] = jnp.broadcast_to(jnp.sum(sums, axis=1, keepdims=True), sums.shape)
    fold_second(3)
    total = res[3]
    for i in range(3):
        got(zres.at[i], z_recv.at[i])
        total = total + zres[i]
    gq_out[...] = total

    for copy in sends:
        copy.wait_send()
    for rd in range(4):
        for o in range(4):
            core_copy(rd, o).wait_send()


def on_device(queries, views, positives, query_weight, owners, view_weight, view_kinds, kind_scale):
    rows, width = queries.shape
    vcols = views.shape[0]
    nchunk = rows // CHUNK
    sub = rows // 64
    half = width // 2
    nrow = rows // 128
    pos = positives.reshape(nrow, 128)
    qw = query_weight.reshape(nrow, 128)
    own = owners.reshape(NPB, 1, vcols)
    vw = view_weight.reshape(NPB, 1, vcols)
    kind = view_kinds.reshape(NPB, 1, vcols)
    vmem = pl.BlockSpec(memory_space=pltpu.VMEM)
    V = pltpu.VMEM
    dma = pltpu.SemaphoreType.DMA
    gq, gv, tg = pl.pallas_call(
        functools.partial(kernel, rows * NPB),
        out_shape=(
            jax.ShapeDtypeStruct((sub, width), F32),
            jax.ShapeDtypeStruct((vcols, width), F32),
            jax.ShapeDtypeStruct((8, 128), F32),
        ),
        in_specs=[pl.BlockSpec(memory_space=pltpu.SMEM), vmem, pl.BlockSpec(memory_space=pl.ANY)] + [vmem] * 5,
        out_specs=(vmem, vmem, vmem),
        scratch_shapes=[
            V((rows, width), BF16),
            V((width, 2 * rows), BF16),
            V((2, 4, 4, 2, sub, width), BF16),
            V((2 * vcols, width), BF16),
            V((2 * rows, 2 * vcols), F32),
            V((2 * rows, 2 * vcols), BF16),
            V((2, sub, width), F32),
            V((2, sub, width), BF16),
            V((2 * nrow, 128), F32),
            V((2 * nrow, 128), F32),
            V((2 * rows, 128), F32),
            V((2 * rows, 128), F32),
            V((2 * rows, 128), F32),
            V((4, NY, NX, sub, width), F32),
            V((4, NY, NX, sub, width), BF16),
            V((4, NY, NX, sub, width), BF16),
            V((4, NX, NY, sub, half), BF16),
            V((4, NY, NX, sub, half), BF16),
            V((4, NX, NY, sub, half), BF16),
            V((4, NY, NX, sub, half), BF16),
            V((4, NY, sub, half), BF16),
            V((4, NX, sub, half), BF16),
            V((4, NY, sub, half), BF16),
            V((4, NX, sub, half), BF16),
            V((4, NY, sub, half), F32),
            V((4, NX, sub, half), F32),
            V((4, sub, width), F32),
            V((3, sub, width), F32),
            V((2, width, vcols), F32),
            V((width, vcols), BF16),
            V((width, vcols), BF16),
            V((2, 2 * nchunk, vcols), F32),
            V((3, nrow, 128), F32),
            V((2, 2, 1, vcols), F32),
            V((2, 1, vcols), F32),
            V((NA, 2, nrow, 128), F32),
            V((NB, 2, nrow, 128), F32),
            V((2, nrow, 128), F32),
            V((NA, 8, 128), F32),
            V((NB, 8, 128), F32),
            V((2, 8, 128), F32),
            dma((nchunk,)), dma((2,)),
            dma((16,)), dma((16,)),
            dma((8,)), dma((8,)),
            dma((4,)), dma((4,)),
            dma((1,)), dma((1,)),
            dma((NA + NB,)), dma((NA + NB,)),
            dma((NA + NB + 1,)), dma((NA + NB + 1,)),
            dma((16,)), dma((16,)),
            dma((64,)), dma((64,)),
            dma((4,)), dma((4,)),
        ],
        compiler_params=pltpu.CompilerParams(collective_id=0, has_side_effects=True,
                                             vmem_limit_bytes=63 * 1024 * 1024),
    )(kind_scale, views, queries.reshape(4, 4, 4, sub, width), pos, qw, own, vw, kind)
    return gq, gv, tg[:3, 0]


def solution(mesh):
    in_specs = (P("pb", None), P(("vert", "pb"), None), P("pb"), P("pb"), P("vert"), P("vert"), P("vert"), P())
    out_specs = (P(("pb", "vert"), None), P(("vert", "pb"), None), P())
    return jax.shard_map(on_device, mesh=mesh, in_specs=in_specs, out_specs=out_specs, check_vma=False)
```

time: 798 us -> 103 us (0.13)
  blocking collectives: 507 us -> 0 us
  waiting for transfers between devices: 201 us -> 0 us
  Pallas kernels: 0 us -> 96 us
  other arithmetic: 38.4 us -> 0 us
  matrix products: 26.8 us -> 0 us
  between operations: 14 us -> 0.64 us
    psum x3 -> x0, blocking collectives: 299 us -> none  [the longest x1 203 us: on_device(): row_sum = lax.psum(row_total * jnp.exp(row_peak - row_max), 'vert')]
    pmax x2 -> x0, blocking collectives: 208 us -> none  [the longest x1 198 us: on_device(): row_max = lax.pmax(row_peak, 'vert')]
    reduce_scatter x2 -> x0, waiting for transfers between devices: 160 us -> none  [the longest x1 160 us: on_device(): lax.psum_scatter(jnp.dot(half_tile, v_half, preferred_element_type=jnp.fl...]
    pallas_call x0 -> x1, Pallas kernels: none -> 96 us  [on_device(): pl.pallas_call(functools.partial(kernel, rows * NPB), out_shape=(jax.Shap...]
    all_gather x1 -> x0, waiting for transfers between devices: 40.8 us -> none  [on_device(): lax.all_gather(views.astype(jnp.bfloat16), 'pb', axis=0, tiled=True)]
    dot_general x6 -> x0, matrix products: 26.8 us -> none  [the longest x4 11 us: scored(): lax.dot_general(q_block, v_half, (((1,), (1,)), ((), ())), preferred_elem...]
    dynamic_update_slice x4 -> x0, other arithmetic: 14.6 us -> none  [on_device(): lax.scan(second_pass, jnp.zeros((tile_cols,), jnp.float32), operands)]
    reduce_sum x10 -> x0, other arithmetic: 13.6 us -> none  [the longest x4 10.5 us: second_pass(): col_terms = col_terms + jnp.sum(grad * scores, axis=0)]
  transfers between devices with their start and end apart: 3 -> 0, of which waited for: 2 -> 0; matrix products, arithmetic and copies ran while one was open for 2% -> 0% of each run, Pallas kernels for 0% -> 0%
where the time goes in v2:
time: 103 us; the launch traced here: 102 us
  Pallas kernels  96 us (93%)
  local copies, waits for them, and re-layouts  4.91 us (5%)
    pallas_call x1, Pallas kernels, on_device(): pl.pallas_call(functools.partial(kernel, rows * NPB), out_shape=(jax.Shap...  96 us
    unnamed x2, local copies, waits for them, and re-layouts  3.6 us

profile of v2, /device:TPU:2, one launch (start us, length us, event | category | flops | bytes accessed | tf_op | source)
XLA Modules:
  0.0 101.5 jit_solution(18274816947858641815)
XLA Ops:
  0.6 96.0 %shard_map.103 = (f32[32,768]{1,0:T(8,128)}, f32[256,768]{1,0:T(8,128)}, f32[8,128]{1,0:T(8,128)}) custom-call(f32[3]{0:T(128)} %kscale_ref.1, f32[256,768]{1,0:T(8,128)} %views_ref.1, f32[4,4,4,32,768]{4,3,2,1,0:T(8,128)} %bitcast.6, s32[16,128]{1,0:T(8,128)} %bitcast.7, f32[16,128]{1,0:T(8,128)} %bitcast.8, s32[4,1,256]{2,1,0:T(1,128)} %bitcast.9, ...), custom_call_target="tpu_custom_call" | custom-call | tf_op jit(solution)/shard_map/pallas_call | solution.py:476
  96.6 1.3 %slice_reduce_fusion = f32[3]{0:T(128)} fusion(f32[8,128]{1,0:T(8,128)} %get-tuple-element.8), kind=kLoop, calls=%fused_computation | loop fusion | bytes 24 | tf_op jit(solution)/shard_map/slice | solution.py:541
  97.9 1.5 %copy.13 = f32[32,768]{1,0:T(8,128)} copy(f32[32,768]{1,0:T(8,128)} %get-tuple-element.12) | data formatting | bytes 196608
  99.4 2.1 %copy.14 = f32[256,768]{1,0:T(8,128)} copy(f32[256,768]{1,0:T(8,128)} %get-tuple-element.13) | data formatting | bytes 1572864

commit v3 on v2

--- a/solution.py
+++ b/solution.py
@@ -15,17 +15,18 @@
 NX = 4
 NY = 4
 NA = 8
-NB = 16
+NB = 8
 CHUNK = 256
 F32 = jnp.float32
 BF16 = jnp.bfloat16
 
 
-def kernel(total_queries, kscale_ref, views_ref, q_hbm, pos_ref, qw_ref, own_ref, vw_ref, kind_ref,
+def kernel(total_queries, kscale_ref, views_hbm, q_hbm, pos_hbm, qw_hbm, own_hbm, vw_hbm, kind_hbm,
            gq_out, gv_out, tg_out,
+           views_ref, pos_ref, qw_ref, own_ref, vw_ref, kind_ref, in_sem,
            qb, qt, qf, vb, S, H, qslice, qzs, pq, pqf, rep, qwrep, posrep, gown, csend, crecv,
            sa1, sb1, ra1, rb1, sa2, sb2, ra2, rb2, acca, accb, res, zres, gvt, zs, zr,
-           colpart, rowpart, colx, colfin, rowa, rowb, rowfin, ta, tb, tp,
+           colpart, rowpart, colx, colfin, rowa, rowb, rowc, rowfin, ta, tb, to, tp,
            qsem, slsem, ag_send, ag_recv, core_send, core_recv, vz_send, vz_recv,
            col_send, col_recv, row_send, row_recv, t_send, t_recv,
            c_send, c_recv, x_send, x_recv, z_send, z_recv):
@@ -40,7 +41,7 @@
     mate = p + 1 - 2 * even
     far = (p + 2) % NPB
     a_me = v % NA
-    b_me = (upper * 2 + zh) * NY + y
+    b_me = upper * NY + y
     rows, width = qb.shape
     nchunk = rows // CHUNK
     vcols = views_ref.shape[0]
@@ -68,6 +69,12 @@
         slices.append(pltpu.make_async_copy(q_hbm.at[sl // 16, (sl // 4) % 4, sl % 4], qslice.at[i], slsem.at[i]))
         slices[-1].start()
 
+    small = [pltpu.make_async_copy(src, dst, in_sem.at[i]) for i, (src, dst) in enumerate((
+        (views_hbm, views_ref), (pos_hbm, pos_ref), (qw_hbm, qw_ref), (own_hbm, own_ref), (vw_hbm, vw_ref),
+        (kind_hbm, kind_ref)))]
+    for copy in small:
+        copy.start()
+
     def load(r):
         part = (r // 2, pl.ds((r % 2) * 2, 2))
         return pltpu.make_async_copy(q_hbm.at[part], gown.at[part], qsem.at[r])
@@ -79,18 +86,21 @@
     peers_b = []
     for d in range(1, NB):
         i = (b_me + d) % NB
-        peers_b.append(((i // 8) * 2 + even, vert_of((i // NY) % 2, i % NY, x, core)))
-    peers = peers_a + peers_b + [(mate, v)]
+        peers_b.append(((i // NY) * 2 + even, vert_of(zh, i % NY, x, core)))
+    over = (p, vert_of(1 - zh, y, x, core))
+    peers = [over] + peers_a + peers_b + [(mate, v)]
     barrier = pltpu.get_barrier_semaphore()
     for dev in peers:
         pl.semaphore_signal(barrier, inc=1, device_id=dev, device_id_type=MESH)
-    vb[0:vcols, :] = views_ref[...].astype(BF16)
     nrow = rows // 128
-    pq[0:nrow, :] = pos_ref[...].astype(F32)
-    pq[nrow:2 * nrow, :] = qw_ref[...]
     for i in range(2):
         slices[i].wait()
         qzs[i] = qslice[i].astype(BF16)
+    for copy in small:
+        copy.wait()
+    vb[0:vcols, :] = views_ref[...].astype(BF16)
+    pq[0:nrow, :] = pos_ref[...].astype(F32)
+    pq[nrow:2 * nrow, :] = qw_ref[...]
     pl.semaphore_wait(barrier, len(peers))
 
     def to_far(i, src, dst):
@@ -170,23 +180,41 @@
     def got(ref, sem):
         remote(ref, ref, sem, sem, here).wait_recv()
 
+    def spread(src, first, dst, at0):
+        for r in range(nrow):
+            dst[at0 + r * 128:at0 + (r + 1) * 128, :] = jnp.broadcast_to(src[first + r:first + r + 1, :], (128, 128)).T
+
+    def slice_a(i, dest, ssem, rsem):
+        go(remote(qf.at[0, y, i, core], qf.at[0, y, i, core], ag_send.at[ssem], ag_recv.at[rsem], dest))
+
+    def slice_b(i, dest, ssem, rsem):
+        go(remote(qf.at[1, x, i, core], qf.at[1, x, i, core], ag_send.at[ssem], ag_recv.at[rsem], dest))
+
+    def second_a(k):
+        i = (x + k) % NX
+        for d in (1, 3, 2):
+            slice_a(i, to_y(d), 8 + k * 4 + d, 8 + y * 4 + i)
+
+    def second_b(k):
+        i = (y + k) % NY
+        for d in (1, 3, 2):
+            slice_b(i, to_x(d), 24 + k * 4 + d, 24 + x * 4 + i)
+
+    own_pass(0, 0, 2)
     got(qf.at[0, y, x, core], vz_recv.at[0])
     for d in (1, 3, 2):
-        go(remote(qf.at[0, y, x, core], qf.at[0, y, x, core], ag_send.at[d], ag_recv.at[x], to_x(d)))
+        slice_a(x, to_x(d), d, x)
+    second_a(0)
     got(qf.at[1, x, y, core], vz_recv.at[1])
     for d in (1, 3, 2):
-        go(remote(qf.at[1, x, y, core], qf.at[1, x, y, core], ag_send.at[4 + d], ag_recv.at[4 + y], to_y(d)))
-
-    own_pass(0, 0, 4)
-
-    for d in (1, 3, 2):
-        got(qf.at[0, y, (x + d) % NX, core], ag_recv.at[(x + d) % NX])
-    for d in (1, 3, 2):
-        go(remote(qf.at[0, y, :, core], qf.at[0, y, :, core], ag_send.at[8 + d], ag_recv.at[8 + y], to_y(d)))
-    for d in (1, 3, 2):
-        got(qf.at[1, x, (y + d) % NY, core], ag_recv.at[4 + (y + d) % NY])
-    for d in (1, 3, 2):
-        go(remote(qf.at[1, x, :, core], qf.at[1, x, :, core], ag_send.at[12 + d], ag_recv.at[12 + x], to_x(d)))
+        slice_b(y, to_y(d), 4 + d, 4 + y)
+    second_b(0)
+    own_pass(0, 2, 8)
+    for k in (1, 3, 2):
+        got(qf.at[0, y, (x + k) % NX, core], ag_recv.at[(x + k) % NX])
+        second_a(k)
+        got(qf.at[1, x, (y + k) % NY, core], ag_recv.at[4 + (y + k) % NY])
+        second_b(k)
 
     def to_twin(h, o):
         part = qf.at[h, o, :, core]
@@ -195,46 +223,39 @@
     def from_twin(h, o):
         got(qf.at[h, o, :, 1 - core], core_recv.at[h * 4 + o])
 
+    def arrive(d):
+        o = (y + d) % NY
+        for k in (0, 1, 3, 2):
+            i = (x + k) % NX
+            got(qf.at[0, o, i, core], ag_recv.at[8 + o * 4 + i])
+        to_twin(0, o)
+        o = (x + d) % NX
+        for k in (0, 1, 3, 2):
+            i = (y + k) % NY
+            got(qf.at[1, o, i, core], ag_recv.at[24 + o * 4 + i])
+        to_twin(1, o)
+
+    def far_step(d):
+        from_twin(0, (y + d) % NY)
+        from_twin(1, (x + d) % NX)
+        far_pass([(0, (y + d) % NY), (1, (x + d) % NX)])
+
     to_twin(0, y)
     to_twin(1, x)
-
-    own_pass(0, 4, 8)
-
-    def spread(src, first, dst, at0):
-        def step(r, carry):
-            at = pl.multiple_of(at0 + r * 128, 128)
-            dst[pl.ds(at, 128), :] = jnp.broadcast_to(src[pl.ds(first + r, 1), :], (128, 128)).T
-            return carry
-
-        lax.fori_loop(0, nrow, step, 0)
-
     spread(pq, 0, posrep, 0)
     spread(pq, nrow, qwrep, 0)
     got(vb.at[pl.ds(vcols, vcols)], vz_recv.at[2])
     own_pass(1, 0, 8)
+    far_step(0)
     got(pqf, vz_recv.at[3])
     spread(pqf, 0, posrep, rows)
     spread(pqf, nrow, qwrep, rows)
-
-    from_twin(0, y)
-    from_twin(1, x)
-    far_pass([(0, y), (1, x)])
-    for d in (1, 3):
-        got(qf.at[0, (y + d) % NY, :, core], ag_recv.at[8 + (y + d) % NY])
-        to_twin(0, (y + d) % NY)
-        got(qf.at[1, (x + d) % NX, :, core], ag_recv.at[12 + (x + d) % NX])
-        to_twin(1, (x + d) % NX)
-    for d in (1, 3):
-        from_twin(0, (y + d) % NY)
-        from_twin(1, (x + d) % NX)
-        far_pass([(0, (y + d) % NY), (1, (x + d) % NX)])
-    got(qf.at[0, (y + 2) % NY, :, core], ag_recv.at[8 + (y + 2) % NY])
-    to_twin(0, (y + 2) % NY)
-    got(qf.at[1, (x + 2) % NX, :, core], ag_recv.at[12 + (x + 2) % NX])
-    to_twin(1, (x + 2) % NX)
-    from_twin(0, (y + 2) % NY)
-    from_twin(1, (x + 2) % NX)
-    far_pass([(0, (y + 2) % NY), (1, (x + 2) % NX)])
+    arrive(1)
+    arrive(3)
+    far_step(1)
+    arrive(2)
+    far_step(3)
+    far_step(2)
 
     def log_sum(parts):
         m = functools.reduce(jnp.maximum, parts)
@@ -270,22 +291,18 @@
         at = even if sl == 0 else 1 - even
         colfin[sl] = log_sum([colx[0, at], colx[1, at]]) - jnp.log2(vw_ref[blocks[sl]])
     collect(rowb, row_recv, NA, b_me, NB)
-    row_lse = log_sum([rowb[i] for i in range(NB)])
-    rowfin[...] = row_lse
+    rowc[0] = log_sum([rowb[i] for i in range(NB)])
+    go(remote(rowc.at[0], rowc.at[1], col_send.at[1], col_recv.at[1], over))
+    got(rowc.at[1], col_recv.at[1])
+    rowfin[...] = log_sum([rowc[0], rowc[1]])
     pqw = (pq, pqf)
     for b in range(2):
         at = upper if b == 0 else 1 - upper
         rowpart[b] = rowfin[at] - jnp.log2(pqw[b][nrow:2 * nrow, :])
 
     def spread_lse(b):
-        def step(i, carry):
-            for j in range(2):
-                r = i * 2 + j
-                at = pl.multiple_of(b * rows + r * 128, 128)
-                rep[pl.ds(at, 128), :] = jnp.broadcast_to(rowpart[b, pl.ds(r, 1), :], (128, 128)).T
-            return carry
-
-        lax.fori_loop(0, nrow // 2, step, 0)
+        for r in range(nrow):
+            rep[b * rows + r * 128:b * rows + (r + 1) * 128, :] = jnp.broadcast_to(rowpart[b, r:r + 1, :], (128, 128)).T
 
     spread_lse(1)
 
@@ -387,9 +404,12 @@
         for d in range(1, NX):
             val = val + rb2[rd, (x + d) % NX].astype(F32)
         res[rd, :, half:] = val
-        if rd < 3:
-            b, z = rounds[rd]
-            go(remote(res.at[rd], zres.at[rd], z_send.at[rd], z_recv.at[rd], (p if b == 0 else far, vert_of(z, y, x, core))))
+        if rd < 2:
+            go(remote(res.at[rd], zres.at[rd], z_send.at[rd], z_recv.at[rd], (far, v)))
+        if rd == 2:
+            got(zres.at[0], z_recv.at[0])
+            res[2] = res[2] + zres[0]
+            go(remote(res.at[2], zres.at[2], z_send.at[2], z_recv.at[2], over))
 
     def grad_views(sl):
         def step(i, carry):
@@ -435,27 +455,36 @@
     fold_first(2)
     fold_second(1)
     collect(tb, t_recv, NA, b_me, NB)
-    tp[even] = functools.reduce(jnp.add, [tb[i] for i in range(NB)])
-    go(remote(tp.at[even], tp.at[even], t_send.at[NA + NB], t_recv.at[NA + NB], (mate, v)))
+    to[0] = functools.reduce(jnp.add, [tb[i] for i in range(NB)])
+    go(remote(to.at[0], to.at[1], t_send.at[NA + NB], t_recv.at[NA + NB], over))
+    fold_second(2)
     fold_first(3)
-    fold_second(2)
     got(zr, z_recv.at[3])
     gv_out[...] = (gvt[0] + zr[...].astype(F32)).T
-    got(tp.at[1 - even], t_recv.at[NA + NB])
-    sums = tp[0] + tp[1]
-    tg_out[...] = jnp.broadcast_to(jnp.sum(sums, axis=1, keepdims=True), sums.shape)
+    got(to.at[1], t_recv.at[NA + NB])
+    tp[0] = to[0] + to[1]
+    go(remote(tp.at[0], tp.at[1], t_send.at[NA + NB + 1], t_recv.at[NA + NB + 1], (mate, v)))
     fold_second(3)
-    total = res[3]
-    for i in range(3):
-        got(zres.at[i], z_recv.at[i])
-        total = total + zres[i]
-    gq_out[...] = total
+    got(tp.at[1], t_recv.at[NA + NB + 1])
+    sums = jnp.sum(tp[0] + tp[1], axis=1, keepdims=True)
+    tg_out[...] = jnp.broadcast_to(sums, tg_out.shape)
+    got(zres.at[1], z_recv.at[1])
+    total = res[3] + zres[1]
+    got(zres.at[2], z_recv.at[2])
+    gq_out[...] = total + zres[2]
 
     for copy in sends:
         copy.wait_send()
     for rd in range(4):
         for o in range(4):
             core_copy(rd, o).wait_send()
+
+
+def hand_over(gq_in, gv_in, tg_in, gq_out, gv_out, tg_out):
+    gq_out[...] = gq_in[...]
+    gv_out[...] = gv_in[...]
+    for i in range(3):
+        tg_out[i] = tg_in[i, 0]
 
 
 def on_device(queries, views, positives, query_weight, owners, view_weight, view_kinds, kind_scale):
@@ -480,9 +509,16 @@
             jax.ShapeDtypeStruct((vcols, width), F32),
             jax.ShapeDtypeStruct((8, 128), F32),
         ),
-        in_specs=[pl.BlockSpec(memory_space=pltpu.SMEM), vmem, pl.BlockSpec(memory_space=pl.ANY)] + [vmem] * 5,
+        in_specs=[pl.BlockSpec(memory_space=pltpu.SMEM)] + [pl.BlockSpec(memory_space=pl.ANY)] * 7,
         out_specs=(vmem, vmem, vmem),
         scratch_shapes=[
+            V((vcols, width), F32),
+            V((nrow, 128), jnp.int32),
+            V((nrow, 128), F32),
+            V((NPB, 1, vcols), jnp.int32),
+            V((NPB, 1, vcols), F32),
+            V((NPB, 1, vcols), jnp.int32),
+            dma((6,)),
             V((rows, width), BF16),
             V((width, 2 * rows), BF16),
             V((2, 4, 4, 2, sub, width), BF16),
@@ -520,17 +556,19 @@
             V((2, 1, vcols), F32),
             V((NA, 2, nrow, 128), F32),
             V((NB, 2, nrow, 128), F32),
+            V((2, 2, nrow, 128), F32),
             V((2, nrow, 128), F32),
             V((NA, 8, 128), F32),
             V((NB, 8, 128), F32),
             V((2, 8, 128), F32),
+            V((2, 8, 128), F32),
             dma((nchunk,)), dma((2,)),
-            dma((16,)), dma((16,)),
+            dma((40,)), dma((40,)),
             dma((8,)), dma((8,)),
             dma((4,)), dma((4,)),
-            dma((1,)), dma((1,)),
+            dma((2,)), dma((2,)),
             dma((NA + NB,)), dma((NA + NB,)),
-            dma((NA + NB + 1,)), dma((NA + NB + 1,)),
+            dma((NA + NB + 2,)), dma((NA + NB + 2,)),
             dma((16,)), dma((16,)),
             dma((64,)), dma((64,)),
             dma((4,)), dma((4,)),
@@ -538,7 +576,17 @@
         compiler_params=pltpu.CompilerParams(collective_id=0, has_side_effects=True,
                                              vmem_limit_bytes=63 * 1024 * 1024),
     )(kind_scale, views, queries.reshape(4, 4, 4, sub, width), pos, qw, own, vw, kind)
-    return gq, gv, tg[:3, 0]
+    smem = pl.BlockSpec(memory_space=pltpu.SMEM)
+    return pl.pallas_call(
+        hand_over,
+        out_shape=(
+            jax.ShapeDtypeStruct(gq.shape, F32),
+            jax.ShapeDtypeStruct(gv.shape, F32),
+            jax.ShapeDtypeStruct(kind_scale.shape, F32),
+        ),
+        in_specs=[vmem, vmem, smem],
+        out_specs=(vmem, vmem, smem),
+    )(gq, gv, tg)
 
 
 def solution(mesh):

time: 103 us -> 94.5 us (0.917)
  the two profiles are of different devices: /device:TPU:2 before, /device:TPU:32 now
where the time goes in v3:
time: 94.5 us; the launch traced here: 94.4 us
  Pallas kernels  93.6 us (99%)
    pallas_call x1, Pallas kernels, on_device(): pl.pallas_call(functools.partial(kernel, rows * NPB), out_shape=(jax.Shap...  91.4 us
    pallas_call x1, Pallas kernels, on_device(): pl.pallas_call(hand_over, out_shape=(jax.ShapeDtypeStruct(gq.shape, F32),...  2.15 us

profile of v3, /device:TPU:32, one launch (start us, length us, event | category | flops | bytes accessed | tf_op | source)
XLA Modules:
  0.0 94.4 jit_solution(15880209346379501387)
XLA Ops:
  0.6 91.4 %shard_map.103 = (f32[32,768]{1,0:T(8,128)}, f32[256,768]{1,0:T(8,128)}, f32[8,128]{1,0:T(8,128)}) custom-call(f32[3]{0:T(128)} %kscale_ref.1, f32[256,768]{1,0:T(8,128)} %views_hbm.1, f32[4,4,4,32,768]{4,3,2,1,0:T(8,128)} %bitcast.6, s32[16,128]{1,0:T(8,128)} %bitcast.7, f32[16,128]{1,0:T(8,128)} %bitcast.8, s32[4,1,256]{2,1,0:T(1,128)} %bitcast.9, ...), custom_call_target="tpu_custom_call" | custom-call | tf_op jit(solution)/shard_map/pallas_call | solution.py:505
  92.1 2.2 %shard_map.104 = (f32[32,768]{1,0:T(8,128)}, f32[256,768]{1,0:T(8,128)}, f32[3]{0:T(128)}) custom-call(f32[32,768]{1,0:T(8,128)} %get-tuple-element.6.gq_in, f32[256,768]{1,0:T(8,128)} %get-tuple-element.7.gv_in, f32[8,128]{1,0:T(8,128)} %get-tuple-element.8.tg_in), custom_call_target="tpu_custom_call" | custom-call | tf_op jit(solution)/shard_map/pallas_call | solution.py:580

commit v4 on v3

--- a/solution.py
+++ b/solution.py
@@ -23,9 +23,9 @@
 
 def kernel(total_queries, kscale_ref, views_hbm, q_hbm, pos_hbm, qw_hbm, own_hbm, vw_hbm, kind_hbm,
            gq_out, gv_out, tg_out,
-           views_ref, pos_ref, qw_ref, own_ref, vw_ref, kind_ref, in_sem,
+           pos_ref, qw_ref, own_ref, vw_ref, kind_ref, in_sem,
            qb, qt, qf, vb, S, H, qslice, qzs, pq, pqf, rep, qwrep, posrep, gown, csend, crecv,
-           sa1, sb1, ra1, rb1, sa2, sb2, ra2, rb2, acca, accb, res, zres, gvt, zs, zr,
+           sa1, sb1, ra1, rb1, sa2, sb2, ra2, rb2, res, zout, zres, gvt, zs, zr,
            colpart, rowpart, colx, colfin, rowa, rowb, rowc, rowfin, ta, tb, to, tp,
            qsem, slsem, ag_send, ag_recv, core_send, core_recv, vz_send, vz_recv,
            col_send, col_recv, row_send, row_recv, t_send, t_recv,
@@ -40,11 +40,11 @@
     upper = p // 2
     mate = p + 1 - 2 * even
     far = (p + 2) % NPB
-    a_me = v % NA
+    a_me = zh * NX + x
     b_me = upper * NY + y
     rows, width = qb.shape
     nchunk = rows // CHUNK
-    vcols = views_ref.shape[0]
+    vcols = own_ref.shape[2]
     half = width // 2
     sub = gown.shape[3]
 
@@ -70,7 +70,7 @@
         slices[-1].start()
 
     small = [pltpu.make_async_copy(src, dst, in_sem.at[i]) for i, (src, dst) in enumerate((
-        (views_hbm, views_ref), (pos_hbm, pos_ref), (qw_hbm, qw_ref), (own_hbm, own_ref), (vw_hbm, vw_ref),
+        (views_hbm, csend.at[0, pl.ds(0, 2)]), (pos_hbm, pos_ref), (qw_hbm, qw_ref), (own_hbm, own_ref), (vw_hbm, vw_ref),
         (kind_hbm, kind_ref)))]
     for copy in small:
         copy.start()
@@ -82,13 +82,18 @@
     for r in range(nchunk):
         load(r).start()
 
-    peers_a = [(p, (v // NA) * NA + (a_me + d) % NA) for d in range(1, NA)]
+    peers_a = []
+    for d in range(1, NA):
+        i = (a_me + d) % NA
+        peers_a.append((p, vert_of(i // NX, y, i % NX, core)))
     peers_b = []
     for d in range(1, NB):
         i = (b_me + d) % NB
         peers_b.append(((i // NY) * 2 + even, vert_of(zh, i % NY, x, core)))
     over = (p, vert_of(1 - zh, y, x, core))
-    peers = [over] + peers_a + peers_b + [(mate, v)]
+    far_over = (far, vert_of(1 - zh, y, x, core))
+    twin = (p, vert_of(zh, y, x, 1 - core))
+    peers = peers_a + peers_b + [twin, (mate, v), far_over]
     barrier = pltpu.get_barrier_semaphore()
     for dev in peers:
         pl.semaphore_signal(barrier, inc=1, device_id=dev, device_id_type=MESH)
@@ -98,7 +103,7 @@
         qzs[i] = qslice[i].astype(BF16)
     for copy in small:
         copy.wait()
-    vb[0:vcols, :] = views_ref[...].astype(BF16)
+    vb[0:vcols, :] = csend[0, 0:2].reshape(vcols, width).astype(BF16)
     pq[0:nrow, :] = pos_ref[...].astype(F32)
     pq[nrow:2 * nrow, :] = qw_ref[...]
     pl.semaphore_wait(barrier, len(peers))
@@ -118,8 +123,6 @@
     def to_y(d):
         return (p, vert_of(zh, (y + d) % NY, x, core))
 
-    twin = (p, vert_of(zh, y, x, 1 - core))
-
     k0, k1, k2 = kscale_ref[0], kscale_ref[1], kscale_ref[2]
     blocks = (p, mate)
 
@@ -135,7 +138,6 @@
         block = gown[r // 2, pl.ds((r % 2) * 2, 2)].reshape(CHUNK, width)
         at = pl.multiple_of(r * CHUNK, CHUNK)
         qb[pl.ds(at, CHUNK), :] = block.astype(BF16)
-        qt[:, pl.ds(at, CHUNK)] = block.T.astype(BF16)
         return carry
 
     lax.fori_loop(0, nchunk, cast_queries, 0)
@@ -175,7 +177,6 @@
             q = qf[h, o].reshape(CHUNK, width)
             at = pl.multiple_of(rows + r * CHUNK, CHUNK)
             score(q, at, r + nchunk, (0, 1), (2, r))
-            qt[:, pl.ds(at, CHUNK)] = q.T
 
     def got(ref, sem):
         remote(ref, ref, sem, sem, here).wait_recv()
@@ -242,14 +243,10 @@
 
     to_twin(0, y)
     to_twin(1, x)
-    spread(pq, 0, posrep, 0)
-    spread(pq, nrow, qwrep, 0)
     got(vb.at[pl.ds(vcols, vcols)], vz_recv.at[2])
     own_pass(1, 0, 8)
     far_step(0)
     got(pqf, vz_recv.at[3])
-    spread(pqf, 0, posrep, rows)
-    spread(pqf, nrow, qwrep, rows)
     arrive(1)
     arrive(3)
     far_step(1)
@@ -274,15 +271,35 @@
             src = (me + d) % n
             got(buf.at[src], rsem.at[base + src])
 
-    rowa[a_me, upper] = log_sum([rowpart[0], rowpart[1]])
-    rowa[a_me, 1 - upper] = rowpart[2]
-    exchange_a(rowa, row_send, row_recv, 0)
+    rowc[0, upper] = log_sum([rowpart[0], rowpart[1]])
+    rowc[0, 1 - upper] = rowpart[2]
+    go(remote(rowc.at[0], rowc.at[1], col_send.at[1], col_recv.at[1], twin))
     for sl in range(2):
         part = colpart[sl]
         m = jnp.max(part, axis=0, keepdims=True)
         at = even if sl == 0 else 1 - even
         colx[even, at] = m + jnp.log2(jnp.sum(jnp.exp2(part - m), axis=0, keepdims=True))
     go(remote(colx.at[even], colx.at[even], col_send.at[0], col_recv.at[0], (mate, v)))
+    got(rowc.at[1], col_recv.at[1])
+    rowa[a_me] = log_sum([rowc[0], rowc[1]])
+    exchange_a(rowa, row_send, row_recv, 0)
+
+    def turn_own(i, carry):
+        for j in range(2):
+            at = pl.multiple_of((i * 2 + j) * CHUNK, CHUNK)
+            qt[:, pl.ds(at, CHUNK)] = qb[pl.ds(at, CHUNK), :].T
+        return carry
+
+    def turn_far(i, carry):
+        for j in range(2):
+            r = i * 2 + j
+            at = pl.multiple_of(rows + r * CHUNK, CHUNK)
+            qt[:, pl.ds(at, CHUNK)] = qf[r // 4, r % 4].reshape(CHUNK, width).T
+        return carry
+
+    lax.fori_loop(0, nchunk // 2, turn_own, 0)
+    spread(pqf, 0, posrep, rows)
+    spread(pqf, nrow, qwrep, rows)
     collect(rowa, row_recv, 0, a_me, NA)
     rowb[b_me] = log_sum([rowa[i] for i in range(NA)])
     exchange_b(rowb, row_send, row_recv, NA)
@@ -290,11 +307,11 @@
     for sl in range(2):
         at = even if sl == 0 else 1 - even
         colfin[sl] = log_sum([colx[0, at], colx[1, at]]) - jnp.log2(vw_ref[blocks[sl]])
+    lax.fori_loop(0, nchunk // 2, turn_far, 0)
+    spread(pq, 0, posrep, 0)
+    spread(pq, nrow, qwrep, 0)
     collect(rowb, row_recv, NA, b_me, NB)
-    rowc[0] = log_sum([rowb[i] for i in range(NB)])
-    go(remote(rowc.at[0], rowc.at[1], col_send.at[1], col_recv.at[1], over))
-    got(rowc.at[1], col_recv.at[1])
-    rowfin[...] = log_sum([rowc[0], rowc[1]])
+    rowfin[...] = log_sum([rowb[i] for i in range(NB)])
     pqw = (pq, pqf)
     for b in range(2):
         at = upper if b == 0 else 1 - upper
@@ -318,7 +335,7 @@
     owners = [own_ref[k] for k in blocks]
     shifts = [colfin[0], colfin[1]]
     col0 = [(v * (NPB * vcols) + k * vcols).astype(F32) for k in blocks]
-    rounds = [(1, 1 - zh), (1, zh), (0, 1 - zh), (0, zh)]
+    rounds = [(1, 1 - zh), (0, 1 - zh), (1, zh), (0, zh)]
 
     def core_copy(rd, o):
         return remote(csend.at[rd, o], crecv.at[rd, o], c_send.at[rd * 4 + o], c_recv.at[rd * 4 + o], twin)
@@ -342,7 +359,7 @@
         acc = jnp.dot(hh, vb[...], preferred_element_type=F32).reshape(NX, 2, sub, width)
         first, second = acc[:, 0], acc[:, 1]
         gown[rd, o] = jnp.where(core == 0, first, second)
-        csend[rd, o] = jnp.where(core == 0, second, first).astype(BF16)
+        csend[rd, o] = jnp.where(core == 0, second, first)
         core_copy(rd, o).start()
         return tuple(out)
 
@@ -355,7 +372,7 @@
         def step(o, carry):
             core_copy(rd, o).wait_recv()
             for i in range(NX):
-                val = gown[rd, o, i] + crecv[rd, o, i].astype(F32)
+                val = gown[rd, o, i] + crecv[rd, o, i]
                 gown[rd, o, i] = val
                 sa1[rd, i, o] = val[:, :half].astype(BF16)
                 sb1[rd, o, i] = val[:, half:].astype(BF16)
@@ -374,7 +391,7 @@
             val = gown[rd, o, x][:, :half]
             for d in range(1, NX):
                 val = val + ra1[rd, (x + d) % NX, o].astype(F32)
-            acca[rd, o] = val
+            gown[rd, o, x, :, 0:half] = val
             sa2[rd, o] = val.astype(BF16)
         for d in (1, 3, 2):
             go(remote(sa2.at[rd, (y + d) % NY], ra2.at[rd, y], x_send.at[rd * 16 + 8 + d], x_recv.at[rd * 16 + 8 + y],
@@ -385,7 +402,7 @@
             val = gown[rd, y, i][:, half:]
             for d in range(1, NY):
                 val = val + rb1[rd, (y + d) % NY, i].astype(F32)
-            accb[rd, i] = val
+            gown[rd, y, i, :, half:width] = val
             sb2[rd, i] = val.astype(BF16)
         for d in (1, 3, 2):
             go(remote(sb2.at[rd, (x + d) % NX], rb2.at[rd, x], x_send.at[rd * 16 + 12 + d],
@@ -394,22 +411,19 @@
     def fold_second(rd):
         for d in (1, 3, 2):
             got(ra2.at[rd, (y + d) % NY], x_recv.at[rd * 16 + 8 + (y + d) % NY])
-        val = acca[rd, y]
+        val = gown[rd, y, x, :, 0:half]
         for d in range(1, NY):
             val = val + ra2[rd, (y + d) % NY].astype(F32)
         res[rd, :, :half] = val
         for d in (1, 3, 2):
             got(rb2.at[rd, (x + d) % NX], x_recv.at[rd * 16 + 12 + (x + d) % NX])
-        val = accb[rd, x]
+        val = gown[rd, y, x, :, half:width]
         for d in range(1, NX):
             val = val + rb2[rd, (x + d) % NX].astype(F32)
         res[rd, :, half:] = val
-        if rd < 2:
-            go(remote(res.at[rd], zres.at[rd], z_send.at[rd], z_recv.at[rd], (far, v)))
-        if rd == 2:
-            got(zres.at[0], z_recv.at[0])
-            res[2] = res[2] + zres[0]
-            go(remote(res.at[2], zres.at[2], z_send.at[2], z_recv.at[2], over))
+        if rd < 3:
+            zout[rd] = res[rd].astype(BF16)
+            go(remote(zout.at[rd], zres.at[rd], z_send.at[rd], z_recv.at[rd], (far_over, over, (far, v))[rd]))
 
     def grad_views(sl):
         def step(i, carry):
@@ -430,48 +444,48 @@
     terms = grad_half(2, 0, terms)
     fold_core(1)
     terms = grad_half(2, 1, terms)
-    fold_first(0)
     terms = grad_half(3, 0, terms)
     fold_core(2)
     terms = grad_half(3, 1, terms)
-    grad_views(1)
-    zs[...] = gvt[1].astype(BF16)
-    go(remote(zs, zr, z_send.at[3], z_recv.at[3], (mate, v)))
-    fold_core(3)
 
     kinds = []
     for t in range(3):
         kinds.append(functools.reduce(jnp.add, [
             jnp.where(tile([kind_ref[k] for k in blocks], h) == t, terms[h], 0.0) for h in range(ntile)]))
-    ta[a_me] = jnp.concatenate(kinds + [jnp.zeros((5, 128), F32)], axis=0) * (LN2 / total_queries)
+    to[0] = jnp.concatenate(kinds + [jnp.zeros((5, 128), F32)], axis=0) * (LN2 / total_queries)
+    go(remote(to.at[0], to.at[1], t_send.at[NA + NB], t_recv.at[NA + NB], twin))
+    fold_first(0)
+    got(to.at[1], t_recv.at[NA + NB])
+    ta[a_me] = to[0] + to[1]
     exchange_a(ta, t_send, t_recv, 0)
-
+    fold_core(3)
+    grad_views(1)
+    zs[...] = gvt[1].astype(BF16)
+    go(remote(zs, zr, z_send.at[3], z_recv.at[3], (mate, v)))
     fold_first(1)
-    grad_views(0)
-    fold_second(0)
     collect(ta, t_recv, 0, a_me, NA)
     tb[b_me] = functools.reduce(jnp.add, [ta[i] for i in range(NA)])
     exchange_b(tb, t_send, t_recv, NA)
+    fold_second(0)
+    grad_views(0)
     fold_first(2)
     fold_second(1)
     collect(tb, t_recv, NA, b_me, NB)
-    to[0] = functools.reduce(jnp.add, [tb[i] for i in range(NB)])
-    go(remote(to.at[0], to.at[1], t_send.at[NA + NB], t_recv.at[NA + NB], over))
+    tp[0] = functools.reduce(jnp.add, [tb[i] for i in range(NB)])
+    go(remote(tp.at[0], tp.at[1], t_send.at[NA + NB + 1], t_recv.at[NA + NB + 1], (mate, v)))
+    fold_first(3)
     fold_second(2)
-    fold_first(3)
     got(zr, z_recv.at[3])
     gv_out[...] = (gvt[0] + zr[...].astype(F32)).T
-    got(to.at[1], t_recv.at[NA + NB])
-    tp[0] = to[0] + to[1]
-    go(remote(tp.at[0], tp.at[1], t_send.at[NA + NB + 1], t_recv.at[NA + NB + 1], (mate, v)))
-    fold_second(3)
     got(tp.at[1], t_recv.at[NA + NB + 1])
     sums = jnp.sum(tp[0] + tp[1], axis=1, keepdims=True)
     tg_out[...] = jnp.broadcast_to(sums, tg_out.shape)
-    got(zres.at[1], z_recv.at[1])
-    total = res[3] + zres[1]
-    got(zres.at[2], z_recv.at[2])
-    gq_out[...] = total + zres[2]
+    fold_second(3)
+    total = res[3]
+    for i in range(3):
+        got(zres.at[i], z_recv.at[i])
+        total = total + zres[i].astype(F32)
+    gq_out[...] = total
 
     for copy in sends:
         copy.wait_send()
@@ -512,7 +526,6 @@
         in_specs=[pl.BlockSpec(memory_space=pltpu.SMEM)] + [pl.BlockSpec(memory_space=pl.ANY)] * 7,
         out_specs=(vmem, vmem, vmem),
         scratch_shapes=[
-            V((vcols, width), F32),
             V((nrow, 128), jnp.int32),
             V((nrow, 128), F32),
             V((NPB, 1, vcols), jnp.int32),
@@ -533,8 +546,8 @@
             V((2 * rows, 128), F32),
             V((2 * rows, 128), F32),
             V((4, NY, NX, sub, width), F32),
-            V((4, NY, NX, sub, width), BF16),
-            V((4, NY, NX, sub, width), BF16),
+            V((4, NY, NX, sub, width), F32),
+            V((4, NY, NX, sub, width), F32),
             V((4, NX, NY, sub, half), BF16),
             V((4, NY, NX, sub, half), BF16),
             V((4, NX, NY, sub, half), BF16),
@@ -543,10 +556,9 @@
             V((4, NX, sub, half), BF16),
             V((4, NY, sub, half), BF16),
             V((4, NX, sub, half), BF16),
-            V((4, NY, sub, half), F32),
-            V((4, NX, sub, half), F32),
             V((4, sub, width), F32),
-            V((3, sub, width), F32),
+            V((3, sub, width), BF16),
+            V((3, sub, width), BF16),
             V((2, width, vcols), F32),
             V((width, vcols), BF16),
             V((width, vcols), BF16),
@@ -575,7 +587,7 @@
         ],
         compiler_params=pltpu.CompilerParams(collective_id=0, has_side_effects=True,
                                              vmem_limit_bytes=63 * 1024 * 1024),
-    )(kind_scale, views, queries.reshape(4, 4, 4, sub, width), pos, qw, own, vw, kind)
+    )(kind_scale, views.reshape(2, 4, sub, width), queries.reshape(4, 4, 4, sub, width), pos, qw, own, vw, kind)
     smem = pl.BlockSpec(memory_space=pltpu.SMEM)
     return pl.pallas_call(
         hand_over,

time: 94.5 us -> 84.3 us (0.89)
  the two profiles are of different devices: /device:TPU:32 before, /device:TPU:2 now
where the time goes in v4:
time: 84.3 us; the launch traced here: 84.1 us
  Pallas kernels  83.3 us (99%)
    pallas_call x1, Pallas kernels, on_device(): pl.pallas_call(functools.partial(kernel, rows * NPB), out_shape=(jax.Shap...  81.1 us
    pallas_call x1, Pallas kernels, on_device(): pl.pallas_call(hand_over, out_shape=(jax.ShapeDtypeStruct(gq.shape, F32),...  2.15 us

profile of v4, /device:TPU:2, one launch (start us, length us, event | category | flops | bytes accessed | tf_op | source)
XLA Modules:
  0.0 84.1 jit_solution(13359065881712571976)
XLA Ops:
  0.6 81.1 %shard_map.103 = (f32[32,768]{1,0:T(8,128)}, f32[256,768]{1,0:T(8,128)}, f32[8,128]{1,0:T(8,128)}) custom-call(f32[3]{0:T(128)} %kscale_ref.1, f32[2,4,32,768]{3,2,1,0:T(8,128)} %bitcast.8, f32[4,4,4,32,768]{4,3,2,1,0:T(8,128)} %bitcast.7, s32[16,128]{1,0:T(8,128)} %bitcast.9, f32[16,128]{1,0:T(8,128)} %bitcast.10, s32[4,1,256]{2,1,0:T(1,128)} %bitcast.11, ...), custom_call_target="tpu_custom_call" | custom-call | tf_op jit(solution)/shard_map/pallas_call | solution.py:519
  81.8 2.2 %shard_map.104 = (f32[32,768]{1,0:T(8,128)}, f32[256,768]{1,0:T(8,128)}, f32[3]{0:T(128)}) custom-call(f32[32,768]{1,0:T(8,128)} %get-tuple-element.6.gq_in, f32[256,768]{1,0:T(8,128)} %get-tuple-element.7.gv_in, f32[8,128]{1,0:T(8,128)} %get-tuple-element.8.tg_in), custom_call_target="tpu_custom_call" | custom-call | tf_op jit(solution)/shard_map/pallas_call | solution.py:592

commit v5 on v4

--- a/solution.py
+++ b/solution.py
@@ -446,6 +446,7 @@
     terms = grad_half(2, 1, terms)
     terms = grad_half(3, 0, terms)
     fold_core(2)
+    fold_first(0)
     terms = grad_half(3, 1, terms)
 
     kinds = []
@@ -454,11 +455,11 @@
             jnp.where(tile([kind_ref[k] for k in blocks], h) == t, terms[h], 0.0) for h in range(ntile)]))
     to[0] = jnp.concatenate(kinds + [jnp.zeros((5, 128), F32)], axis=0) * (LN2 / total_queries)
     go(remote(to.at[0], to.at[1], t_send.at[NA + NB], t_recv.at[NA + NB], twin))
-    fold_first(0)
     got(to.at[1], t_recv.at[NA + NB])
     ta[a_me] = to[0] + to[1]
     exchange_a(ta, t_send, t_recv, 0)
     fold_core(3)
+    fold_second(0)
     grad_views(1)
     zs[...] = gvt[1].astype(BF16)
     go(remote(zs, zr, z_send.at[3], z_recv.at[3], (mate, v)))
@@ -466,7 +467,6 @@
     collect(ta, t_recv, 0, a_me, NA)
     tb[b_me] = functools.reduce(jnp.add, [ta[i] for i in range(NA)])
     exchange_b(tb, t_send, t_recv, NA)
-    fold_second(0)
     grad_views(0)
     fold_first(2)
     fold_second(1)

time: 84.3 us -> 91.2 us (1.082)
  Pallas kernels: 83.3 us -> 90.3 us
    pallas_call x1, Pallas kernels: 81.1 us -> 88.1 us  [on_device(): pl.pallas_call(functools.partial(kernel, rows * NPB), out_shape=(jax.Shap...]
where the time goes in v5:
time: 91.2 us; the launch traced here: 91.1 us
  Pallas kernels  90.3 us (99%)
    pallas_call x1, Pallas kernels, on_device(): pl.pallas_call(functools.partial(kernel, rows * NPB), out_shape=(jax.Shap...  88.1 us
    pallas_call x1, Pallas kernels, on_device(): pl.pallas_call(hand_over, out_shape=(jax.ShapeDtypeStruct(gq.shape, F32),...  2.15 us

profile of v5, /device:TPU:2, one launch (start us, length us, event | category | flops | bytes accessed | tf_op | source)
XLA Modules:
  0.0 91.1 jit_solution(9868469766321726872)
XLA Ops:
  0.6 88.1 %shard_map.103 = (f32[32,768]{1,0:T(8,128)}, f32[256,768]{1,0:T(8,128)}, f32[8,128]{1,0:T(8,128)}) custom-call(f32[3]{0:T(128)} %kscale_ref.1, f32[2,4,32,768]{3,2,1,0:T(8,128)} %bitcast.8, f32[4,4,4,32,768]{4,3,2,1,0:T(8,128)} %bitcast.7, s32[16,128]{1,0:T(8,128)} %bitcast.9, f32[16,128]{1,0:T(8,128)} %bitcast.10, s32[4,1,256]{2,1,0:T(1,128)} %bitcast.11, ...), custom_call_target="tpu_custom_call" | custom-call | tf_op jit(solution)/shard_map/pallas_call | solution.py:519
  88.8 2.2 %shard_map.104 = (f32[32,768]{1,0:T(8,128)}, f32[256,768]{1,0:T(8,128)}, f32[3]{0:T(128)}) custom-call(f32[32,768]{1,0:T(8,128)} %get-tuple-element.6.gq_in, f32[256,768]{1,0:T(8,128)} %get-tuple-element.7.gv_in, f32[8,128]{1,0:T(8,128)} %get-tuple-element.8.tg_in), custom_call_target="tpu_custom_call" | custom-call | tf_op jit(solution)/shard_map/pallas_call | solution.py:592
